TPU v7x, 256 devices: a whole 4x4x8 slice. The times are simulated.
256 devices in a mesh: seq: 16 (over y, x_lo, core), head: 16 (over x_hi, z).
Axes of the slice: x: 4 (x_hi: 2, x_lo: 2; x = x_hi * 2 + x_lo), y: 4, z: 8, core: 2. Of those that a mesh axis runs over, the one named last changes fastest.
Arguments:
- queries: bfloat16 [16384, 4096], P('seq', 'head'), may hold values from -8 to 8
- key_states: bfloat16 [2048, 4096], P('seq', 'head'), may hold values from -8 to 8
- value_states: bfloat16 [2048, 4096], P('seq', 'head'), may hold values from -6 to 6
- grad_out: bfloat16 [16384, 4096], P('seq', 'head'), may hold values from -6 to 6
- key_weight: bfloat16 [4096, 4096], P(None, 'head'), may hold values from -0.09375 to 0.09375
- value_weight: bfloat16 [4096, 4096], P(None, 'head'), may hold values from -0.09375 to 0.09375
- wait_lag: int32 [1], replicated, may hold values from 1 to 255
- target_offset: int32 [16], replicated, may hold values from 0 to 15360, as said below
- source_offset: int32 [16], replicated, may hold values from 0 to 1920, as said below
Outputs:
- query_grad: bfloat16 [16384, 4096], P('seq', 'head')
- memory_grad: bfloat16 [2048, 4096], P('seq', 'head')
Inputs may be any that keep to these rules, and one draw needn't show every extreme that they name: `target_offset`: each entry is 1024 times a block number, every block number once. `source_offset`: each entry is 128 times a block number, every block number once.
All inputs are finite; a program needn't handle non-finite values.
Results may differ from a plain program's by a relative error of at most 0.0058.
Values may be sent and summed in bfloat16 or wider, within the bound.
A program may use at most 128 MiB of HBM per device.

v0:
```python
import jax
import jax.numpy as jnp
from jax import lax
from jax.sharding import PartitionSpec as P

HEAD_DIM = 64


very_negative = -1e30


def passed_along(value, axis, steps):
    count = lax.axis_size(axis)
    pairs = [(source, (source + steps) % count) for source in range(count)]
    return lax.ppermute(value, axis, pairs)


def positions(offsets, first_row, block_rows, block_size):
    row_ids = first_row + jnp.arange(block_rows, dtype=jnp.int32)
    block_ids = row_ids // block_size
    slot_ids = jnp.arange(offsets.shape[0], dtype=jnp.int32)
    block_base = jnp.sum(
        jnp.where(block_ids[:, None] == slot_ids[None, :], offsets[None, :], 0), axis=1
    )
    return block_base + row_ids % block_size


def body(
    queries,
    key_states,
    value_states,
    grad_out,
    key_weight,
    value_weight,
    wait_lag,
    target_offset,
    source_offset,
):
    query_rows, features = queries.shape
    source_rows = key_states.shape[0]
    head_count = features // HEAD_DIM
    block_count = lax.axis_size("seq")
    own_index = lax.axis_index("seq")
    score_scale = HEAD_DIM ** (-0.5)
    target_ratio = query_rows // source_rows
    query_heads = queries.reshape(query_rows, head_count, HEAD_DIM)
    grad_heads = grad_out.reshape(query_rows, head_count, HEAD_DIM)
    target_pos = positions(target_offset, own_index * query_rows, query_rows, query_rows)
    reach_limit = target_ratio * wait_lag[0] + target_pos

    def visible(first_row, block_rows):
        source_pos = positions(source_offset, first_row, block_rows, source_rows)
        return target_ratio * source_pos[None, :] <= reach_limit[:, None]

    def logits_of(key_block, value_block):
        key_heads = key_block.reshape(key_block.shape[0], head_count, HEAD_DIM)
        value_heads = value_block.reshape(value_block.shape[0], head_count, HEAD_DIM)
        logit_block = (
            jnp.einsum("thc,shc->hts", query_heads, key_heads, preferred_element_type=jnp.float32)
            * score_scale
        )
        grad_probs = jnp.einsum(
            "thc,shc->hts", grad_heads, value_heads, preferred_element_type=jnp.float32
        )
        return (logit_block, grad_probs, key_heads)

    def backward_part(key_block, value_block, first_row, log_total, row_dots):
        block_rows = key_block.shape[0]
        allowed = visible(first_row, block_rows)[None]
        logit_block, grad_probs, key_heads = logits_of(key_block, value_block)
        prob_block = jnp.where(allowed, jnp.exp(logit_block - log_total[:, :, None]), 0.0)
        score_grad = prob_block * (grad_probs - row_dots[:, :, None])
        prob_half = prob_block.astype(jnp.bfloat16)
        grad_half = score_grad.astype(jnp.bfloat16)
        value_term = jnp.einsum(
            "hts,thc->shc", prob_half, grad_heads, preferred_element_type=jnp.float32
        )
        key_term = (
            jnp.einsum("hts,thc->shc", grad_half, query_heads, preferred_element_type=jnp.float32)
            * score_scale
        )
        query_term = (
            jnp.einsum("hts,shc->thc", grad_half, key_heads, preferred_element_type=jnp.float32)
            * score_scale
        )
        return (
            query_term.reshape(query_rows, features),
            key_term.reshape(block_rows, features),
            value_term.reshape(block_rows, features),
        )

    query_zero = jnp.zeros((query_rows, features), jnp.float32)
    source_zero = jnp.zeros((source_rows, features), jnp.float32)
    key_block = lax.all_gather(key_states, "seq", axis=0, tiled=True)
    value_block = lax.all_gather(value_states, "seq", axis=0, tiled=True)
    allowed = visible(jnp.int32(0), key_block.shape[0])[None]
    running_max = jnp.full((head_count, query_rows), very_negative, jnp.float32)
    logit_block, grad_probs, key_heads = logits_of(key_block, value_block)
    block_max = jnp.max(jnp.where(allowed, logit_block, very_negative), axis=2)
    new_max = jnp.maximum(running_max, block_max)
    prob_block = jnp.where(allowed, jnp.exp(logit_block - new_max[:, :, None]), 0.0)
    running_sum = jnp.sum(prob_block, axis=2)
    running_dot = jnp.sum(prob_block * grad_probs, axis=2)
    log_total = new_max + jnp.log(running_sum)
    row_dots = running_dot / running_sum

    def rotate_turn(turn_index, carried):
        key_block, value_block, key_total, value_total, query_total = carried
        owner = (own_index - turn_index) % block_count
        query_term, key_term, value_term = backward_part(
            key_block, value_block, owner * source_rows, log_total, row_dots
        )
        key_total = key_total + key_term
        value_total = value_total + value_term
        key_block, value_block = passed_along((key_block, value_block), "seq", 1)
        key_total, value_total = passed_along((key_total, value_total), "seq", 1)
        return (key_block, value_block, key_total, value_total, query_total + query_term)

    finished = lax.fori_loop(
        0,
        block_count,
        rotate_turn,
        (key_states, value_states, source_zero, source_zero, query_zero),
    )
    key_grad = finished[2]
    value_grad = finished[3]
    query_total = finished[4]
    key_half = key_grad.astype(jnp.bfloat16)
    value_half = value_grad.astype(jnp.bfloat16)
    contract = (((1,), (1,)), ((), ()))
    partial_memory = lax.dot_general(
        key_half, key_weight, contract, preferred_element_type=jnp.float32
    )
    partial_memory = partial_memory + lax.dot_general(
        value_half, value_weight, contract, preferred_element_type=jnp.float32
    )
    memory_grad = lax.psum_scatter(partial_memory, "head", scatter_dimension=1, tiled=True).astype(
        jnp.bfloat16
    )
    return (query_total.astype(jnp.bfloat16), memory_grad)


def solution(mesh):
    in_specs = (
        P("seq", "head"),
        P("seq", "head"),
        P("seq", "head"),
        P("seq", "head"),
        P(None, "head"),
        P(None, "head"),
        P(),
        P(),
        P(),
    )
    out_specs = (P("seq", "head"), P("seq", "head"))
    return jax.shard_map(body, mesh=mesh, in_specs=in_specs, out_specs=out_specs, check_vma=False)
```

profile of v0, /device:TPU:32, one launch (start us, length us, event | category | flops | bytes accessed | tf_op | source)
XLA Modules:
  0.0 613.6 jit_solution(6260983308017984032)
XLA Ops:
  15.4 2.1 copy.20
  18.1 3.0 broadcast_compare_fusion.1
  21.2 26.3 %all-gather.3.cloned.1.call-done = bf16[2048,256]{1,0:T(8,128)(2,1)} async-done(((bf16[128,256]{1,0:T(8,128)(2,1)}), bf16[2048,256]{1,0:T(8,128)(2,1)}) %all-gather.3.cloned.1.call-update) | async-done | bytes 1048592 | tf_op jit(solution)/shard_map/all_gather | solution.py:94
  49.0 15.7 %select_reduce_fusion.1 = (f32[4,1024]{1,0:T(4,128)S(1)}, f32[4,1024,2048]{2,1,0:T(8,128)}) fusion(pred[1024,2048]{1,0:T(8,128)(4,1)} %broadcast_compare_fusion.1, bf16[1024,4,64]{0,2,1:T(8,128)(2,1)} %bitcast.1, bf16[2048,4,64]{0,2,1:T(8,128)(2,1)S(1)} %bitcast.66), kind=kOutput, calls=%fused_computation.22 | convolution fusion | flops 1098903552 | bytes 37240832 | tf_op jit(solution)/shard_map/thc,shc->hts/dot_general | solution.py:59
  64.7 15.2 %fusion.4 = f32[4,1024]{1,0:T(4,128)S(1)} fusion(f32[4,1024,2048]{2,1,0:T(8,128)} %get-tuple-element.456, f32[4,1024]{1,0:T(4,128)S(1)} %broadcast_maximum_fusion, pred[1024,2048]{1,0:T(8,128)(4,1)S(1)} %copy-done.2), kind=kLoop, calls=%fused_computation.23 | loop fusion | flops 33550336 | bytes 35684352 | tf_op jit(solution)/shard_map/reduce_sum | solution.py:102
  79.9 4.6 all-gather.5.cloned.1.call-done
  86.0 16.3 %multiply_reduce_fusion = f32[4,1024]{1,0:T(4,128)S(1)} fusion(f32[4,1024,2048]{2,1,0:T(8,128)} %get-tuple-element.456, bf16[1024,4,64]{0,2,1:T(8,128)(2,1)} %bitcast.3, bf16[2048,4,64]{0,2,1:T(8,128)(2,1)S(1)} %bitcast.65, f32[4,1024]{1,0:T(4,128)S(1)} %broadcast_maximum_fusion, pred[1024,2048]{1,0:T(8,128)(4,1)} %broadcast_compare_fusion.1), kind=kOutput, calls=%fused_computation.20 | convolution fusion | flops 1115680768 | bytes 37257216 | tf_op jit(solution)/shard_map/thc,shc->hts/dot_general | solution.py:62
  103.0 292.0 %while.25 = (s32[]{:T(128)}, bf16[128,256]{0,1:T(8,128)(2,1)}, bf16[128,256]{0,1:T(8,128)(2,1)}, f32[128,256]{0,1:T(8,128)S(1)}, f32[128,256]{0,1:T(8,128)S(1)},...) while((s32[]{:T(128)}, bf16[128,256]{0,1:T(8,128)(2,1)}, ...), condition=%wide.region_7.8_spmd.clone, body=%wide.region_5.7_spmd.clone.sunk | while | flops 340240000 | bytes 19111452 | solution.py:119
  120.5 2.3 collective-permute-done.3
  136.1 2.5 bitcast_add_fusion.8
  153.7 2.5 bitcast_add_fusion.8
  157.0 2.0 collective-permute-done.3
  171.8 2.5 bitcast_add_fusion.8
  189.4 2.5 bitcast_add_fusion.8
  193.3 2.0 collective-permute-done.3
  207.9 2.5 bitcast_add_fusion.8
  226.4 2.5 bitcast_add_fusion.8
  245.0 2.5 bitcast_add_fusion.8
  247.7 2.0 collective-permute-done.3
  263.1 2.5 bitcast_add_fusion.8
  281.3 2.5 bitcast_add_fusion.8
  284.0 2.0 collective-permute-done.3
  299.4 2.5 bitcast_add_fusion.8
  317.6 2.5 bitcast_add_fusion.8
  320.3 2.0 collective-permute-done.3
  335.7 2.5 bitcast_add_fusion.8
  353.9 2.5 bitcast_add_fusion.8
  372.0 2.5 bitcast_add_fusion.8
  374.8 2.0 collective-permute-done.3
  390.2 2.5 bitcast_add_fusion.8
  396.6 2.2 convolution_add_fusion
  401.0 204.6 %reduce-scatter.2.cloned.1.call-done = f32[128,256]{1,0:T(8,128)} async-done(((f32[128,4096]{1,0:T(8,128)}), f32[128,256]{1,0:T(8,128)}) %reduce-scatter.2.cloned.1.call-update) | async-done | bytes 131088 | tf_op jit(solution)/shard_map/reduce_scatter | solution.py:137
  (365 shorter events, 256.6 us)
Async XLA Ops:
  7.2 40.3 %all-gather.3.cloned.1.call-start = ((), (), s32[]{:S(2)}) async-start(), calls=%async_computation.1 | async-start | bytes 1114112 | tf_op jit(solution)/shard_map/all_gather | solution.py:94
  7.9 76.6 %all-gather.5.cloned.1.call-start = ((), (), s32[]{:S(2)}) async-start(), calls=%async_computation.2 | async-start | bytes 1114112 | tf_op jit(solution)/shard_map/all_gather | solution.py:95
  8.7 596.9 %reduce-scatter.2.cloned.1.call-start = ((), (), s32[]{:S(2)}) async-start(), calls=%async_computation.3 | async-start | bytes 2228224 | tf_op jit(solution)/shard_map/reduce_scatter | solution.py:137
  104.0 15.1 %collective-permute-start = (bf16[128,256]{0,1:T(8,128)(2,1)S(1)}, bf16[128,256]{0,1:T(8,128)(2,1)}, u32[]{:S(2)}, u32[]{:S(2)}) collective-permute-start(bf16[128,256]{0,1:T(8,128)(2,1)S(1)} %copy.32), channel_id=1, source_target_pairs={{0,16},{16,32},{32,48},{48,64},{64,80},{80,96},{96,112},{112,128},... | collective-permute-start | bytes 196616 | tf_op jit(solution)/shard_map/while/body/eval_jaxpr/ppermute | solution.py:15
  105.1 14.1 %collective-permute-start.1 = (bf16[128,256]{0,1:T(8,128)(2,1)S(1)}, bf16[128,256]{0,1:T(8,128)(2,1)}, u32[]{:S(2)}, u32[]{:S(2)}) collective-permute-start(bf16[128,256]{0,1:T(8,128)(2,1)S(1)} %copy.33), channel_id=1, source_target_pairs={{0,16},{16,32},{32,48},{48,64},{64,80},{80,96},{96,112},{112,128},... | collective-permute-start | bytes 196616 | tf_op jit(solution)/shard_map/while/body/eval_jaxpr/ppermute | solution.py:15
  123.6 14.9 %collective-permute-start = (bf16[128,256]{0,1:T(8,128)(2,1)S(1)}, bf16[128,256]{0,1:T(8,128)(2,1)}, u32[]{:S(2)}, u32[]{:S(2)}) collective-permute-start(bf16[128,256]{0,1:T(8,128)(2,1)S(1)} %copy.32), channel_id=1, source_target_pairs={{0,16},{16,32},{32,48},{48,64},{64,80},{80,96},{96,112},{112,128},... | collective-permute-start | bytes 196616 | tf_op jit(solution)/shard_map/while/body/eval_jaxpr/ppermute | solution.py:15
  124.4 14.1 %collective-permute-start.1 = (bf16[128,256]{0,1:T(8,128)(2,1)S(1)}, bf16[128,256]{0,1:T(8,128)(2,1)}, u32[]{:S(2)}, u32[]{:S(2)}) collective-permute-start(bf16[128,256]{0,1:T(8,128)(2,1)S(1)} %copy.33), channel_id=1, source_target_pairs={{0,16},{16,32},{32,48},{48,64},{64,80},{80,96},{96,112},{112,128},... | collective-permute-start | bytes 196616 | tf_op jit(solution)/shard_map/while/body/eval_jaxpr/ppermute | solution.py:15
  141.7 14.4 %collective-permute-start = (bf16[128,256]{0,1:T(8,128)(2,1)S(1)}, bf16[128,256]{0,1:T(8,128)(2,1)}, u32[]{:S(2)}, u32[]{:S(2)}) collective-permute-start(bf16[128,256]{0,1:T(8,128)(2,1)S(1)} %copy.32), channel_id=1, source_target_pairs={{0,16},{16,32},{32,48},{48,64},{64,80},{80,96},{96,112},{112,128},... | collective-permute-start | bytes 196616 | tf_op jit(solution)/shard_map/while/body/eval_jaxpr/ppermute | solution.py:15
  159.9 14.4 %collective-permute-start = (bf16[128,256]{0,1:T(8,128)(2,1)S(1)}, bf16[128,256]{0,1:T(8,128)(2,1)}, u32[]{:S(2)}, u32[]{:S(2)}) collective-permute-start(bf16[128,256]{0,1:T(8,128)(2,1)S(1)} %copy.32), channel_id=1, source_target_pairs={{0,16},{16,32},{32,48},{48,64},{64,80},{80,96},{96,112},{112,128},... | collective-permute-start | bytes 196616 | tf_op jit(solution)/shard_map/while/body/eval_jaxpr/ppermute | solution.py:15
  160.7 13.6 %collective-permute-start.1 = (bf16[128,256]{0,1:T(8,128)(2,1)S(1)}, bf16[128,256]{0,1:T(8,128)(2,1)}, u32[]{:S(2)}, u32[]{:S(2)}) collective-permute-start(bf16[128,256]{0,1:T(8,128)(2,1)S(1)} %copy.33), channel_id=1, source_target_pairs={{0,16},{16,32},{32,48},{48,64},{64,80},{80,96},{96,112},{112,128},... | collective-permute-start | bytes 196616 | tf_op jit(solution)/shard_map/while/body/eval_jaxpr/ppermute | solution.py:15
  178.0 13.9 %collective-permute-start = (bf16[128,256]{0,1:T(8,128)(2,1)S(1)}, bf16[128,256]{0,1:T(8,128)(2,1)}, u32[]{:S(2)}, u32[]{:S(2)}) collective-permute-start(bf16[128,256]{0,1:T(8,128)(2,1)S(1)} %copy.32), channel_id=1, source_target_pairs={{0,16},{16,32},{32,48},{48,64},{64,80},{80,96},{96,112},{112,128},... | collective-permute-start | bytes 196616 | tf_op jit(solution)/shard_map/while/body/eval_jaxpr/ppermute | solution.py:15
  196.2 14.2 %collective-permute-start = (bf16[128,256]{0,1:T(8,128)(2,1)S(1)}, bf16[128,256]{0,1:T(8,128)(2,1)}, u32[]{:S(2)}, u32[]{:S(2)}) collective-permute-start(bf16[128,256]{0,1:T(8,128)(2,1)S(1)} %copy.32), channel_id=1, source_target_pairs={{0,16},{16,32},{32,48},{48,64},{64,80},{80,96},{96,112},{112,128},... | collective-permute-start | bytes 196616 | tf_op jit(solution)/shard_map/while/body/eval_jaxpr/ppermute | solution.py:15
  214.3 14.6 %collective-permute-start = (bf16[128,256]{0,1:T(8,128)(2,1)S(1)}, bf16[128,256]{0,1:T(8,128)(2,1)}, u32[]{:S(2)}, u32[]{:S(2)}) collective-permute-start(bf16[128,256]{0,1:T(8,128)(2,1)S(1)} %copy.32), channel_id=1, source_target_pairs={{0,16},{16,32},{32,48},{48,64},{64,80},{80,96},{96,112},{112,128},... | collective-permute-start | bytes 196616 | tf_op jit(solution)/shard_map/while/body/eval_jaxpr/ppermute | solution.py:15
  215.2 13.7 %collective-permute-start.1 = (bf16[128,256]{0,1:T(8,128)(2,1)S(1)}, bf16[128,256]{0,1:T(8,128)(2,1)}, u32[]{:S(2)}, u32[]{:S(2)}) collective-permute-start(bf16[128,256]{0,1:T(8,128)(2,1)S(1)} %copy.33), channel_id=1, source_target_pairs={{0,16},{16,32},{32,48},{48,64},{64,80},{80,96},{96,112},{112,128},... | collective-permute-start | bytes 196616 | tf_op jit(solution)/shard_map/while/body/eval_jaxpr/ppermute | solution.py:15
  232.5 15.0 %collective-permute-start = (bf16[128,256]{0,1:T(8,128)(2,1)S(1)}, bf16[128,256]{0,1:T(8,128)(2,1)}, u32[]{:S(2)}, u32[]{:S(2)}) collective-permute-start(bf16[128,256]{0,1:T(8,128)(2,1)S(1)} %copy.32), channel_id=1, source_target_pairs={{0,16},{16,32},{32,48},{48,64},{64,80},{80,96},{96,112},{112,128},... | collective-permute-start | bytes 196616 | tf_op jit(solution)/shard_map/while/body/eval_jaxpr/ppermute | solution.py:15
  233.3 14.1 %collective-permute-start.1 = (bf16[128,256]{0,1:T(8,128)(2,1)S(1)}, bf16[128,256]{0,1:T(8,128)(2,1)}, u32[]{:S(2)}, u32[]{:S(2)}) collective-permute-start(bf16[128,256]{0,1:T(8,128)(2,1)S(1)} %copy.33), channel_id=1, source_target_pairs={{0,16},{16,32},{32,48},{48,64},{64,80},{80,96},{96,112},{112,128},... | collective-permute-start | bytes 196616 | tf_op jit(solution)/shard_map/while/body/eval_jaxpr/ppermute | solution.py:15
  250.6 15.0 %collective-permute-start = (bf16[128,256]{0,1:T(8,128)(2,1)S(1)}, bf16[128,256]{0,1:T(8,128)(2,1)}, u32[]{:S(2)}, u32[]{:S(2)}) collective-permute-start(bf16[128,256]{0,1:T(8,128)(2,1)S(1)} %copy.32), channel_id=1, source_target_pairs={{0,16},{16,32},{32,48},{48,64},{64,80},{80,96},{96,112},{112,128},... | collective-permute-start | bytes 196616 | tf_op jit(solution)/shard_map/while/body/eval_jaxpr/ppermute | solution.py:15
  251.5 14.1 %collective-permute-start.1 = (bf16[128,256]{0,1:T(8,128)(2,1)S(1)}, bf16[128,256]{0,1:T(8,128)(2,1)}, u32[]{:S(2)}, u32[]{:S(2)}) collective-permute-start(bf16[128,256]{0,1:T(8,128)(2,1)S(1)} %copy.33), channel_id=1, source_target_pairs={{0,16},{16,32},{32,48},{48,64},{64,80},{80,96},{96,112},{112,128},... | collective-permute-start | bytes 196616 | tf_op jit(solution)/shard_map/while/body/eval_jaxpr/ppermute | solution.py:15
  268.8 15.0 %collective-permute-start = (bf16[128,256]{0,1:T(8,128)(2,1)S(1)}, bf16[128,256]{0,1:T(8,128)(2,1)}, u32[]{:S(2)}, u32[]{:S(2)}) collective-permute-start(bf16[128,256]{0,1:T(8,128)(2,1)S(1)} %copy.32), channel_id=1, source_target_pairs={{0,16},{16,32},{32,48},{48,64},{64,80},{80,96},{96,112},{112,128},... | collective-permute-start | bytes 196616 | tf_op jit(solution)/shard_map/while/body/eval_jaxpr/ppermute | solution.py:15
  269.6 14.1 %collective-permute-start.1 = (bf16[128,256]{0,1:T(8,128)(2,1)S(1)}, bf16[128,256]{0,1:T(8,128)(2,1)}, u32[]{:S(2)}, u32[]{:S(2)}) collective-permute-start(bf16[128,256]{0,1:T(8,128)(2,1)S(1)} %copy.33), channel_id=1, source_target_pairs={{0,16},{16,32},{32,48},{48,64},{64,80},{80,96},{96,112},{112,128},... | collective-permute-start | bytes 196616 | tf_op jit(solution)/shard_map/while/body/eval_jaxpr/ppermute | solution.py:15
  286.9 15.0 %collective-permute-start = (bf16[128,256]{0,1:T(8,128)(2,1)S(1)}, bf16[128,256]{0,1:T(8,128)(2,1)}, u32[]{:S(2)}, u32[]{:S(2)}) collective-permute-start(bf16[128,256]{0,1:T(8,128)(2,1)S(1)} %copy.32), channel_id=1, source_target_pairs={{0,16},{16,32},{32,48},{48,64},{64,80},{80,96},{96,112},{112,128},... | collective-permute-start | bytes 196616 | tf_op jit(solution)/shard_map/while/body/eval_jaxpr/ppermute | solution.py:15
  287.8 14.1 %collective-permute-start.1 = (bf16[128,256]{0,1:T(8,128)(2,1)S(1)}, bf16[128,256]{0,1:T(8,128)(2,1)}, u32[]{:S(2)}, u32[]{:S(2)}) collective-permute-start(bf16[128,256]{0,1:T(8,128)(2,1)S(1)} %copy.33), channel_id=1, source_target_pairs={{0,16},{16,32},{32,48},{48,64},{64,80},{80,96},{96,112},{112,128},... | collective-permute-start | bytes 196616 | tf_op jit(solution)/shard_map/while/body/eval_jaxpr/ppermute | solution.py:15
  305.1 15.0 %collective-permute-start = (bf16[128,256]{0,1:T(8,128)(2,1)S(1)}, bf16[128,256]{0,1:T(8,128)(2,1)}, u32[]{:S(2)}, u32[]{:S(2)}) collective-permute-start(bf16[128,256]{0,1:T(8,128)(2,1)S(1)} %copy.32), channel_id=1, source_target_pairs={{0,16},{16,32},{32,48},{48,64},{64,80},{80,96},{96,112},{112,128},... | collective-permute-start | bytes 196616 | tf_op jit(solution)/shard_map/while/body/eval_jaxpr/ppermute | solution.py:15
  305.9 14.1 %collective-permute-start.1 = (bf16[128,256]{0,1:T(8,128)(2,1)S(1)}, bf16[128,256]{0,1:T(8,128)(2,1)}, u32[]{:S(2)}, u32[]{:S(2)}) collective-permute-start(bf16[128,256]{0,1:T(8,128)(2,1)S(1)} %copy.33), channel_id=1, source_target_pairs={{0,16},{16,32},{32,48},{48,64},{64,80},{80,96},{96,112},{112,128},... | collective-permute-start | bytes 196616 | tf_op jit(solution)/shard_map/while/body/eval_jaxpr/ppermute | solution.py:15
  323.2 15.0 %collective-permute-start = (bf16[128,256]{0,1:T(8,128)(2,1)S(1)}, bf16[128,256]{0,1:T(8,128)(2,1)}, u32[]{:S(2)}, u32[]{:S(2)}) collective-permute-start(bf16[128,256]{0,1:T(8,128)(2,1)S(1)} %copy.32), channel_id=1, source_target_pairs={{0,16},{16,32},{32,48},{48,64},{64,80},{80,96},{96,112},{112,128},... | collective-permute-start | bytes 196616 | tf_op jit(solution)/shard_map/while/body/eval_jaxpr/ppermute | solution.py:15
  324.1 14.1 %collective-permute-start.1 = (bf16[128,256]{0,1:T(8,128)(2,1)S(1)}, bf16[128,256]{0,1:T(8,128)(2,1)}, u32[]{:S(2)}, u32[]{:S(2)}) collective-permute-start(bf16[128,256]{0,1:T(8,128)(2,1)S(1)} %copy.33), channel_id=1, source_target_pairs={{0,16},{16,32},{32,48},{48,64},{64,80},{80,96},{96,112},{112,128},... | collective-permute-start | bytes 196616 | tf_op jit(solution)/shard_map/while/body/eval_jaxpr/ppermute | solution.py:15
  341.4 15.0 %collective-permute-start = (bf16[128,256]{0,1:T(8,128)(2,1)S(1)}, bf16[128,256]{0,1:T(8,128)(2,1)}, u32[]{:S(2)}, u32[]{:S(2)}) collective-permute-start(bf16[128,256]{0,1:T(8,128)(2,1)S(1)} %copy.32), channel_id=1, source_target_pairs={{0,16},{16,32},{32,48},{48,64},{64,80},{80,96},{96,112},{112,128},... | collective-permute-start | bytes 196616 | tf_op jit(solution)/shard_map/while/body/eval_jaxpr/ppermute | solution.py:15
  342.2 14.1 %collective-permute-start.1 = (bf16[128,256]{0,1:T(8,128)(2,1)S(1)}, bf16[128,256]{0,1:T(8,128)(2,1)}, u32[]{:S(2)}, u32[]{:S(2)}) collective-permute-start(bf16[128,256]{0,1:T(8,128)(2,1)S(1)} %copy.33), channel_id=1, source_target_pairs={{0,16},{16,32},{32,48},{48,64},{64,80},{80,96},{96,112},{112,128},... | collective-permute-start | bytes 196616 | tf_op jit(solution)/shard_map/while/body/eval_jaxpr/ppermute | solution.py:15
  359.5 15.0 %collective-permute-start = (bf16[128,256]{0,1:T(8,128)(2,1)S(1)}, bf16[128,256]{0,1:T(8,128)(2,1)}, u32[]{:S(2)}, u32[]{:S(2)}) collective-permute-start(bf16[128,256]{0,1:T(8,128)(2,1)S(1)} %copy.32), channel_id=1, source_target_pairs={{0,16},{16,32},{32,48},{48,64},{64,80},{80,96},{96,112},{112,128},... | collective-permute-start | bytes 196616 | tf_op jit(solution)/shard_map/while/body/eval_jaxpr/ppermute | solution.py:15
  360.4 14.1 %collective-permute-start.1 = (bf16[128,256]{0,1:T(8,128)(2,1)S(1)}, bf16[128,256]{0,1:T(8,128)(2,1)}, u32[]{:S(2)}, u32[]{:S(2)}) collective-permute-start(bf16[128,256]{0,1:T(8,128)(2,1)S(1)} %copy.33), channel_id=1, source_target_pairs={{0,16},{16,32},{32,48},{48,64},{64,80},{80,96},{96,112},{112,128},... | collective-permute-start | bytes 196616 | tf_op jit(solution)/shard_map/while/body/eval_jaxpr/ppermute | solution.py:15
  377.7 15.0 %collective-permute-start = (bf16[128,256]{0,1:T(8,128)(2,1)S(1)}, bf16[128,256]{0,1:T(8,128)(2,1)}, u32[]{:S(2)}, u32[]{:S(2)}) collective-permute-start(bf16[128,256]{0,1:T(8,128)(2,1)S(1)} %copy.32), channel_id=1, source_target_pairs={{0,16},{16,32},{32,48},{48,64},{64,80},{80,96},{96,112},{112,128},... | collective-permute-start | bytes 196616 | tf_op jit(solution)/shard_map/while/body/eval_jaxpr/ppermute | solution.py:15
  378.5 14.1 %collective-permute-start.1 = (bf16[128,256]{0,1:T(8,128)(2,1)S(1)}, bf16[128,256]{0,1:T(8,128)(2,1)}, u32[]{:S(2)}, u32[]{:S(2)}) collective-permute-start(bf16[128,256]{0,1:T(8,128)(2,1)S(1)} %copy.33), channel_id=1, source_target_pairs={{0,16},{16,32},{32,48},{48,64},{64,80},{80,96},{96,112},{112,128},... | collective-permute-start | bytes 196616 | tf_op jit(solution)/shard_map/while/body/eval_jaxpr/ppermute | solution.py:15
  (40 other events, 671.3 us)
Sparse Core Ops, SparseCore 0:
  9.9 37.5 all-gather.2
  49.4 35.0 all-gather.4
  398.9 206.5 reduce-scatter.1
where the time goes:
time: 621 us; the launch traced here: 614 us
  waiting for transfers between devices  279 us (45%)
  matrix products  151 us (24%)
  other arithmetic  107 us (17%)
  local copies, waits for them, and re-layouts  40.1 us (6%)
  starting transfers between devices  20.9 us (3%)
  between operations  14.5 us (2%)
    reduce_scatter x1, waiting for transfers between devices, body(): lax.psum_scatter(partial_memory, 'head', scatter_dimension=1, tiled=True)  205 us
    dot_general x17, matrix products, logits_of(): jnp.einsum('thc,shc->hts', grad_heads, value_heads, preferred_element_typ...  48.2 us
    dot_general x17, matrix products, logits_of(): jnp.einsum('thc,shc->hts', query_heads, key_heads, preferred_element_type...  47.9 us
    ppermute x64, waiting for transfers between devices, passed_along(): return lax.ppermute(value, axis, pairs)  42.2 us
    add x16, other arithmetic, rotate_turn(): query_total + query_term  38.1 us
    while x32, local copies, waits for them, and re-layouts  26.9 us
    all_gather x1, waiting for transfers between devices, body(): key_block = lax.all_gather(key_states, 'seq', axis=0, tiled=True)  26.3 us
    dot_general x16, matrix products, backward_part(): jnp.einsum('hts,thc->shc', prob_half, grad_heads, preferred_element_type=...  22 us
  transfers between devices with their start and end apart: 67, of which 35 were waited for; matrix products, arithmetic and copies ran while one was open for 42% of the time, Pallas kernels for 0%

commit v1 on v0

v1 whole, which is shorter than its diff:
```python
import functools

import jax
import jax.numpy as jnp
from jax import lax
from jax.experimental import pallas as pl
from jax.experimental.pallas import tpu as pltpu
from jax.sharding import PartitionSpec as P

F32 = jnp.float32
BF16 = jnp.bfloat16
NEG = -1e30
HEADS, HD, TGT, SRC, SB, RATIO = 4, 64, 1024, 2048, 128, 8
FEAT = HEADS * HD
TILE = 512
CHUNK = 256
CHIPS = SRC // CHUNK
COLS = 256
NZ = 8
FAR_FIRST = (4, 3, 5, 2, 6, 1, 7, 0)
MESH = pl.DeviceIdType.MESH


def kernel(lag, toff, soff, q, g, k, v, wk_hbm, wv_hbm, dq, mem,
           qT, gT, qz, gz, kv, kT, s_ref, dp_ref, e_ref, acc, ds, dqT, part, sib, mid, rs, wk, wv, xs, xr, zs, zr,
           ag_s, ag_r, fw_s, fw_r, sb_s, sb_r, rs_s, rs_r, x_s, x_r, z_s, z_r, w_sem):
    me, head = lax.axis_index("seq"), lax.axis_index("head")
    y, xl, core = me // 4, lax.rem(me // 2, 2), lax.rem(me, 2)
    chip = me // 2
    xh, z = head // NZ, lax.rem(head, NZ)
    sibling = (chip * 2 + 1 - core, head)
    partner = (me, (1 - xh) * NZ + z)

    def chip_at(r, sign):
        return lax.rem(y + sign * (r // 2) + 4, 4) * 2 + (1 - xl if r % 2 else xl)

    def peer(r):
        return (chip_at(r, 1) * 2 + core, head)

    def z_at(r):
        return lax.rem(z + r, NZ)

    def z_peer(r):
        return (me, xh * NZ + z_at(r))

    barrier = pltpu.get_barrier_semaphore()
    for other in [sibling, partner] + [peer(r) for r in range(1, CHIPS)] + [z_peer(r) for r in range(1, NZ)]:
        pl.semaphore_signal(barrier, inc=1, device_id=other, device_id_type=MESH)

    def remote(src, dst, s_sem, r_sem, dev):
        return pltpu.make_async_remote_copy(src_ref=src, dst_ref=dst, send_sem=s_sem, recv_sem=r_sem, device_id=dev, device_id_type=MESH)

    def gather_out(h, r):
        return remote(kv.at[h, chip, core], kv.at[h, chip, core], ag_s.at[h, r], ag_r.at[h, r], peer(r))

    def gather_in(h, r):
        there = kv.at[h, chip_at(r, -1), core]
        return remote(there, there, ag_s.at[h, r], ag_r.at[h, r], peer(r))

    def forward(h):
        return remote(kv.at[h, :, core], kv.at[h, :, core], fw_s.at[h], fw_r.at[h], sibling)

    def forward_in(h):
        return remote(kv.at[h, :, 1 - core], kv.at[h, :, 1 - core], fw_s.at[h], fw_r.at[h], sibling)

    def to_sibling(h):
        return remote(part.at[h, :, 1 - core], sib.at[h], sb_s.at[h], sb_r.at[h], sibling)

    def scatter_out(h, r):
        return remote(mid.at[h, chip_at(r, 1)], rs.at[h, r], rs_s.at[h, r], rs_r.at[h, r], peer(r))

    def across(r):
        return remote(xs.at[r], xr.at[r], x_s.at[r], x_r.at[r], partner)

    def along(r):
        return remote(zs.at[r], zr.at[r], z_s.at[r], z_r.at[r], z_peer(r))

    load_k = pltpu.make_async_copy(wk_hbm, wk, w_sem.at[0])
    load_v = pltpu.make_async_copy(wv_hbm, wv, w_sem.at[1])
    load_k.start()
    load_v.start()

    low = lax.broadcasted_iota(jnp.int32, (1, 128), 1) < HD

    def swapped(a):
        return jnp.concatenate([a[:, HD:], a[:, :HD]], axis=1)

    for p in range(HEADS // 2):
        kp, vp = k[:, p * 128 : (p + 1) * 128], v[:, p * 128 : (p + 1) * 128]
        kv[2 * p, chip, core] = jnp.where(low, kp, swapped(vp))
        kv[2 * p + 1, chip, core] = jnp.where(low, swapped(kp), vp)

    pl.semaphore_wait(barrier, 16)
    for h in range(HEADS):
        for r in range(1, CHIPS):
            gather_out(h, r).start()

    for p in range(HEADS // 2):
        qp = q[:, p * 128 : (p + 1) * 128] * jnp.asarray(HD**-0.5, BF16)
        gp = g[:, p * 128 : (p + 1) * 128]
        qt, gt = qp.T, gp.T
        none = jnp.zeros_like(qp)
        zero = jnp.zeros((HD, TGT), BF16)
        qs, gs = swapped(qp), swapped(gp)
        for j in range(2):
            h = p * 2 + j
            qz[h] = jnp.where(low, qs if j else qp, none)
            gz[h] = jnp.where(low, none, gp if j else gs)
            qT[h, :HD, :] = qt[j * HD : (j + 1) * HD]
            qT[h, HD:, :] = zero
            gT[h, :HD, :] = zero
            gT[h, HD:, :] = gt[j * HD : (j + 1) * HD]

    def take_gathered(h):
        for r in range(1, CHIPS):
            gather_in(h, r).wait_recv()
        forward(h).start()

    def keys_ready(h):
        forward_in(h).wait_recv()
        kT[h] = kv[h].reshape(SRC, 128).T[:HD]

    def mid_step(h):
        to_sibling(h).wait_recv()
        mid[h] = (part[h, :, core].astype(F32) + sib[h].astype(F32)).astype(BF16)
        for r in range(1, CHIPS):
            scatter_out(h, r).start()

    take_gathered(0)
    keys_ready(0)

    def tile(h, i):
        ts = pl.ds(pl.multiple_of(i * TILE, TILE), TILE)
        reach = RATIO * lag[0] + toff[me] + i * TILE + lax.broadcasted_iota(jnp.int32, (1, TILE), 1)
        qt, gt = qT[h, :, ts], gT[h, :, ts]
        m = jnp.full((8, TILE), NEG, F32)
        for c in range(CHIPS):
            s = jnp.dot(kv[h, c].reshape(CHUNK, 128), qt, preferred_element_type=F32)
            for b in range(2):
                block = 2 * c + b
                pos = RATIO * soff[block] + RATIO * lax.broadcasted_iota(jnp.int32, (SB, TILE), 0)
                sb = jnp.where(pos <= reach, s[b * SB : (b + 1) * SB], NEG)
                s_ref[block * SB : (block + 1) * SB, :] = sb
                m = jnp.maximum(m, jnp.max(sb.reshape(SB // 8, 8, TILE), axis=0))
        m1 = jnp.max(m, axis=0, keepdims=True)
        l = jnp.zeros((8, TILE), F32)
        d = jnp.zeros((8, TILE), F32)
        for c in range(CHIPS):
            cs = slice(c * CHUNK, (c + 1) * CHUNK)
            dp = jnp.dot(kv[h, c].reshape(CHUNK, 128), gt, preferred_element_type=F32)
            e = jnp.exp(s_ref[cs, :] - m1)
            l = l + jnp.sum(e.reshape(CHUNK // 8, 8, TILE), axis=0)
            d = d + jnp.sum((e * dp).reshape(CHUNK // 8, 8, TILE), axis=0)
            e_ref[cs, :] = e
            dp_ref[cs, :] = dp
        inv = 1.0 / jnp.sum(l, axis=0, keepdims=True)
        dots = jnp.sum(d, axis=0, keepdims=True) * inv
        qzt, gzt = qz[h, ts, :], gz[h, ts, :]
        for c in range(CHIPS):
            cs = slice(c * CHUNK, (c + 1) * CHUNK)
            prob = e_ref[cs, :] * inv
            grad = (prob * (dp_ref[cs, :] - dots)).astype(BF16)
            ds[h, cs, ts] = grad
            acc[cs, :] += jnp.dot(prob.astype(BF16), gzt, preferred_element_type=F32) + jnp.dot(grad, qzt, preferred_element_type=F32)

    def query_grad(h):
        dqT[h] = jnp.dot(kT[h], ds[h], preferred_element_type=F32) * HD**-0.5

    @pl.loop(0, HEADS)
    def _(h):
        acc[...] = jnp.zeros_like(acc)

        @pl.loop(0, TGT // TILE)
        def _(i):
            @pl.when(i == 1)
            def _():
                @pl.when(h < HEADS - 1)
                def _():
                    take_gathered(h + 1)

                @pl.when(h > 0)
                def _():
                    mid_step(h - 1)

            tile(h, i)

        part[h] = acc[...].astype(BF16).reshape(CHIPS, 2, SB, 128)
        to_sibling(h).start()

        @pl.when(h < HEADS - 1)
        def _():
            keys_ready(h + 1)

    query_grad(0)
    mid_step(HEADS - 1)

    @pl.loop(1, HEADS)
    def _(h):
        query_grad(h)

    half = []
    for h in range(HEADS):
        total = mid[h, chip].astype(F32)
        for r in range(1, CHIPS):
            scatter_out(h, r).wait_recv()
            total = total + rs[h, r].astype(F32)
        half.append(total)

    half_k = jnp.concatenate([jnp.where(low, half[2 * p], swapped(half[2 * p + 1])) for p in range(2)], axis=1).astype(BF16)
    half_v = jnp.concatenate([jnp.where(low, swapped(half[2 * p]), half[2 * p + 1]) for p in range(2)], axis=1).astype(BF16)
    load_k.wait()
    load_v.wait()
    contract = (((1,), (1,)), ((), ()))

    def term(index):
        rows = pl.ds(pl.multiple_of(index * COLS, COLS), COLS)
        return lax.dot_general(half_k, wk[rows, :], contract, preferred_element_type=F32) + lax.dot_general(
            half_v, wv[rows, :], contract, preferred_element_type=F32
        )

    for r in FAR_FIRST:
        xs[r] = term((1 - xh) * NZ + z_at(r)).astype(BF16)
        across(r).start()
    for r in FAR_FIRST:
        own = term(xh * NZ + z_at(r))
        across(r).wait_recv()
        own = own + xr[r].astype(F32)
        if r:
            zs[r] = own.astype(BF16)
            along(r).start()
        else:
            total = own
    dq[...] = dqT[...].reshape(FEAT, TGT).T.astype(BF16)
    for r in (1, 7, 2, 6, 3, 5, 4):
        along(r).wait_recv()
        total = total + zr[r].astype(F32)
    mem[...] = total.astype(BF16)

    for h in range(HEADS):
        for r in range(1, CHIPS):
            gather_out(h, r).wait_send()
            scatter_out(h, r).wait_send()
        forward(h).wait_send()
        to_sibling(h).wait_send()
    for r in range(NZ):
        across(r).wait_send()
        if r:
            along(r).wait_send()


def attention(lag, toff, soff, q, g, k, v, wk, wv):
    vmem, smem, dma = pltpu.VMEM, pltpu.SMEM, pltpu.SemaphoreType.DMA
    return pl.pallas_call(
        kernel,
        out_shape=(jax.ShapeDtypeStruct((TGT, FEAT), BF16), jax.ShapeDtypeStruct((SB, COLS), BF16)),
        in_specs=[pl.BlockSpec(memory_space=smem)] * 3
        + [pl.BlockSpec(memory_space=vmem)] * 4
        + [pl.BlockSpec(memory_space=pl.ANY)] * 2,
        out_specs=(pl.BlockSpec(memory_space=vmem),) * 2,
        scratch_shapes=[
            vmem((HEADS, 128, TGT), BF16),
            vmem((HEADS, 128, TGT), BF16),
            vmem((HEADS, TGT, 128), BF16),
            vmem((HEADS, TGT, 128), BF16),
            vmem((HEADS, CHIPS, 2, SB, 128), BF16),
            vmem((HEADS, HD, SRC), BF16),
            vmem((SRC, TILE), F32),
            vmem((SRC, TILE), F32),
            vmem((SRC, TILE), F32),
            vmem((SRC, 128), F32),
            vmem((HEADS, SRC, TGT), BF16),
            vmem((HEADS, HD, TGT), F32),
            vmem((HEADS, CHIPS, 2, SB, 128), BF16),
            vmem((HEADS, CHIPS, SB, 128), BF16),
            vmem((HEADS, CHIPS, SB, 128), BF16),
            vmem((HEADS, CHIPS, SB, 128), BF16),
            vmem((16 * COLS, FEAT), BF16),
            vmem((16 * COLS, FEAT), BF16),
        ]
        + [vmem((NZ, SB, COLS), BF16)] * 4
        + [dma((HEADS, CHIPS))] * 2
        + [dma((HEADS,))] * 4
        + [dma((HEADS, CHIPS))] * 2
        + [dma((NZ,))] * 4
        + [dma((2,))],
        compiler_params=pltpu.CompilerParams(vmem_limit_bytes=58 * 2**20, collective_id=0, has_side_effects=True),
        name="wait_k_backward",
    )(lag, toff, soff, q, g, k, v, wk, wv)


def body(queries, key_states, value_states, grad_out, key_weight, value_weight, wait_lag, target_offset, source_offset):
    return attention(wait_lag, target_offset, source_offset, queries, grad_out, key_states, value_states, key_weight, value_weight)


def solution(mesh):
    rows = P("seq", "head")
    in_specs = (rows, rows, rows, rows, P(None, "head"), P(None, "head"), P(), P(), P())
    return jax.shard_map(body, mesh=mesh, in_specs=in_specs, out_specs=(rows, rows), check_vma=False)
```

time: 621 us -> 80.9 us (0.13); the launches traced: 614 us -> 80 us
  waiting for transfers between devices: 279 us -> 0 us
  matrix products: 151 us -> 0 us
  other arithmetic: 107 us -> 0 us
  Pallas kernels: 0 us -> 75.4 us
  local copies, waits for them, and re-layouts: 40.1 us -> 3.34 us
  starting transfers between devices: 20.9 us -> 0 us
  between operations: 14.5 us -> 1.29 us
    reduce_scatter x1 -> x0, waiting for transfers between devices: 205 us -> none  [body(): lax.psum_scatter(partial_memory, 'head', scatter_dimension=1, tiled=True)]
    dot_general x84 -> x0, matrix products: 151 us -> none  [the longest x17 48.2 us: logits_of(): jnp.einsum('thc,shc->hts', grad_heads, value_heads, preferred_element_typ...]
    pallas_call x0 -> x1, Pallas kernels: none -> 75.4 us  [attention(): pl.pallas_call(kernel, out_shape=(jax.ShapeDtypeStruct((TGT, FEAT), BF16)...]
    add x49 -> x0, other arithmetic: 59.8 us -> none  [the longest x16 38.1 us: rotate_turn(): query_total + query_term]
    ppermute x64 -> x0, waiting for transfers between devices: 42.2 us -> none  [passed_along(): return lax.ppermute(value, axis, pairs)]
    all_gather x2 -> x0, waiting for transfers between devices: 30.9 us -> none  [the longest x1 26.3 us: body(): key_block = lax.all_gather(key_states, 'seq', axis=0, tiled=True)]
    reduce_sum x19 -> x0, other arithmetic: 28 us -> none  [the longest x1 15.2 us: body(): running_sum = jnp.sum(prob_block, axis=2)]
    while x33 -> x0, local copies, waits for them, and re-layouts: 27.9 us -> none
  transfers between devices with their start and end apart: 67 -> 0, of which waited for: 35 -> 0; matrix products, arithmetic and copies ran while one was open for 42% -> 0% of each run, Pallas kernels for 0% -> 0%
where the time goes in v1:
time: 80.9 us; the launch traced here: 80 us
  Pallas kernels  75.4 us (93%)
  local copies, waits for them, and re-layouts  3.34 us (4%)
  between operations  1.29 us (2%)
    pallas_call x1, Pallas kernels, attention(): pl.pallas_call(kernel, out_shape=(jax.ShapeDtypeStruct((TGT, FEAT), BF16)...  75.4 us
    unnamed x2, local copies, waits for them, and re-layouts  3.34 us

profile of v1, /device:TPU:32, one launch (start us, length us, event | category | flops | bytes accessed | tf_op | source)
XLA Modules:
  0.0 80.0 jit_solution(2542548451884659406)
XLA Ops:
  1.3 75.4 %wait_k_backward.1 = (bf16[1024,256]{1,0:T(8,128)(2,1)}, bf16[128,256]{1,0:T(8,128)(2,1)}) custom-call(s32[1]{0:T(128)S(6)} %copy.13.lag, s32[16]{0:T(128)} %toff.1, s32[16]{0:T(128)} %soff.1, bf16[1024,256]{1,0:T(8,128)(2,1)} %q.1, bf16[1024,256]{1,0:T(8,128)(2,1)} %g.1, bf16[128,256]{1,0:T(8,128)(2,1)} %k.1, bf16[128,256]{1,0:T(8,128)(2,1)} %v.1, ...), custom_call_target="tpu_custom_call" | custom-call | tf_op jit(solution)/shard_map/wait_k_backward/pallas_call | solution.py:253
  76.7 1.9 %copy.14 = bf16[1024,256]{1,0:T(8,128)(2,1)} copy(bf16[1024,256]{1,0:T(8,128)(2,1)} %get-tuple-element.4) | data formatting | bytes 1048576
  78.5 1.5 %copy.15 = bf16[128,256]{1,0:T(8,128)(2,1)} copy(bf16[128,256]{1,0:T(8,128)(2,1)} %get-tuple-element.5) | data formatting | bytes 131072

commit v2 on v1

--- a/solution.py
+++ b/solution.py
@@ -12,18 +12,20 @@
 NEG = -1e30
 HEADS, HD, TGT, SRC, SB, RATIO = 4, 64, 1024, 2048, 128, 8
 FEAT = HEADS * HD
-TILE = 512
+TILE = 256
+TILES = TGT // TILE
 CHUNK = 256
 CHIPS = SRC // CHUNK
 COLS = 256
 NZ = 8
 FAR_FIRST = (4, 3, 5, 2, 6, 1, 7, 0)
+NEAR = (1, 7, 2, 6)
 MESH = pl.DeviceIdType.MESH
 
 
 def kernel(lag, toff, soff, q, g, k, v, wk_hbm, wv_hbm, dq, mem,
-           qT, gT, qz, gz, kv, kT, s_ref, dp_ref, e_ref, acc, ds, dqT, part, sib, mid, rs, wk, wv, xs, xr, zs, zr,
-           ag_s, ag_r, fw_s, fw_r, sb_s, sb_r, rs_s, rs_r, x_s, x_r, z_s, z_r, w_sem):
+           qT, gT, qz, gz, kv, kT, e_a, d_a, m_a, e_b, d_b, m_b, dots, acc, own, ds, dqT, part, sib, mid, rs, wk, wv, xs, xr, zs, zr, zl,
+           ag_s, ag_r, fw_s, fw_r, sb_s, sb_r, rs_s, rs_r, x_s, x_r, z_s, z_r, l_r, w_sem):
     me, head = lax.axis_index("seq"), lax.axis_index("head")
     y, xl, core = me // 4, lax.rem(me // 2, 2), lax.rem(me, 2)
     chip = me // 2
@@ -44,7 +46,7 @@
         return (me, xh * NZ + z_at(r))
 
     barrier = pltpu.get_barrier_semaphore()
-    for other in [sibling, partner] + [peer(r) for r in range(1, CHIPS)] + [z_peer(r) for r in range(1, NZ)]:
+    for other in [sibling, partner] + [peer(r) for r in range(1, CHIPS)] + [z_peer(r) for r in NEAR]:
         pl.semaphore_signal(barrier, inc=1, device_id=other, device_id_type=MESH)
 
     def remote(src, dst, s_sem, r_sem, dev):
@@ -74,6 +76,10 @@
 
     def along(r):
         return remote(zs.at[r], zr.at[r], z_s.at[r], z_r.at[r], z_peer(r))
+
+    def relay(r):
+        step = 2 + 4 * core if r == 4 else 1 if r == 3 else 7
+        return remote(zs.at[r], zl.at[r - 3], z_s.at[r], l_r.at[r - 3], z_peer(step))
 
     load_k = pltpu.make_async_copy(wk_hbm, wk, w_sem.at[0])
     load_v = pltpu.make_async_copy(wv_hbm, wv, w_sem.at[1])
@@ -90,12 +96,7 @@
         kv[2 * p, chip, core] = jnp.where(low, kp, swapped(vp))
         kv[2 * p + 1, chip, core] = jnp.where(low, swapped(kp), vp)
 
-    pl.semaphore_wait(barrier, 16)
-    for h in range(HEADS):
-        for r in range(1, CHIPS):
-            gather_out(h, r).start()
-
-    for p in range(HEADS // 2):
+    def prepare(p):
         qp = q[:, p * 128 : (p + 1) * 128] * jnp.asarray(HD**-0.5, BF16)
         gp = g[:, p * 128 : (p + 1) * 128]
         qt, gt = qp.T, gp.T
@@ -111,6 +112,12 @@
             gT[h, :HD, :] = zero
             gT[h, HD:, :] = gt[j * HD : (j + 1) * HD]
 
+    prepare(0)
+    pl.semaphore_wait(barrier, 13)
+    for r in range(1, CHIPS):
+        gather_out(0, r).start()
+    prepare(1)
+
     def take_gathered(h):
         for r in range(1, CHIPS):
             gather_in(h, r).wait_recv()
@@ -118,61 +125,101 @@
 
     def keys_ready(h):
         forward_in(h).wait_recv()
-        kT[h] = kv[h].reshape(SRC, 128).T[:HD]
 
     def mid_step(h):
         to_sibling(h).wait_recv()
-        mid[h] = (part[h, :, core].astype(F32) + sib[h].astype(F32)).astype(BF16)
+        mid[h] = (own[...] + sib[h].astype(F32)).astype(BF16)
         for r in range(1, CHIPS):
             scatter_out(h, r).start()
 
     take_gathered(0)
+
+    @pl.loop(1, HEADS)
+    def _(h):
+        for r in range(1, CHIPS):
+            gather_out(h, r).start()
+
     keys_ready(0)
 
-    def tile(h, i):
+    def first_half(h, i, e_ref, d_ref, m_ref):
         ts = pl.ds(pl.multiple_of(i * TILE, TILE), TILE)
         reach = RATIO * lag[0] + toff[me] + i * TILE + lax.broadcasted_iota(jnp.int32, (1, TILE), 1)
+        step = RATIO * lax.broadcasted_iota(jnp.int32, (SB, TILE), 0)
         qt, gt = qT[h, :, ts], gT[h, :, ts]
         m = jnp.full((8, TILE), NEG, F32)
-        for c in range(CHIPS):
-            s = jnp.dot(kv[h, c].reshape(CHUNK, 128), qt, preferred_element_type=F32)
-            for b in range(2):
-                block = 2 * c + b
-                pos = RATIO * soff[block] + RATIO * lax.broadcasted_iota(jnp.int32, (SB, TILE), 0)
-                sb = jnp.where(pos <= reach, s[b * SB : (b + 1) * SB], NEG)
-                s_ref[block * SB : (block + 1) * SB, :] = sb
-                m = jnp.maximum(m, jnp.max(sb.reshape(SB // 8, 8, TILE), axis=0))
-        m1 = jnp.max(m, axis=0, keepdims=True)
         l = jnp.zeros((8, TILE), F32)
         d = jnp.zeros((8, TILE), F32)
         for c in range(CHIPS):
-            cs = slice(c * CHUNK, (c + 1) * CHUNK)
-            dp = jnp.dot(kv[h, c].reshape(CHUNK, 128), gt, preferred_element_type=F32)
-            e = jnp.exp(s_ref[cs, :] - m1)
-            l = l + jnp.sum(e.reshape(CHUNK // 8, 8, TILE), axis=0)
-            d = d + jnp.sum((e * dp).reshape(CHUNK // 8, 8, TILE), axis=0)
-            e_ref[cs, :] = e
-            dp_ref[cs, :] = dp
-        inv = 1.0 / jnp.sum(l, axis=0, keepdims=True)
-        dots = jnp.sum(d, axis=0, keepdims=True) * inv
+            both = kv[h, c].reshape(CHUNK, 128)
+            s = jnp.dot(both, qt, preferred_element_type=F32)
+            dp = jnp.dot(both, gt, preferred_element_type=F32)
+            for b in range(2):
+                block = 2 * c + b
+                rows = slice(block * SB, (block + 1) * SB)
+                seen = jnp.where(step <= reach - RATIO * soff[block], s[b * SB : (b + 1) * SB], NEG).reshape(SB // 8, 8, TILE)
+                grads = dp[b * SB : (b + 1) * SB].reshape(SB // 8, 8, TILE)
+                new = jnp.maximum(m, jnp.max(seen, axis=0))
+                scale = jnp.exp(m - new)
+                e = jnp.exp(seen - new[None])
+                l = l * scale + jnp.sum(e, axis=0)
+                d = d * scale + jnp.sum(e * grads, axis=0)
+                m = new
+                e_ref[rows, :] = e.reshape(SB, TILE)
+                d_ref[rows, :] = grads.reshape(SB, TILE)
+                m_ref[block] = m
+            yield
+        top = jnp.max(m, axis=0, keepdims=True)
+        weight = jnp.exp(m - top)
+        inv = 1.0 / jnp.sum(l * weight, axis=0, keepdims=True)
+        yield jnp.broadcast_to(jnp.sum(d * weight, axis=0, keepdims=True) * inv, (8, TILE))
+        for block in range(2 * CHIPS):
+            m_ref[block] = jnp.exp(m_ref[block] - top) * inv
+
+    def second_half(h, i, e_ref, d_ref, m_ref, dot):
+        ts = pl.ds(pl.multiple_of(i * TILE, TILE), TILE)
         qzt, gzt = qz[h, ts, :], gz[h, ts, :]
         for c in range(CHIPS):
+            probs, grads = [], []
+            for b in range(2):
+                block = 2 * c + b
+                rows = slice(block * SB, (block + 1) * SB)
+                prob = e_ref[rows, :].reshape(SB // 8, 8, TILE) * m_ref[block][None]
+                grad = prob * (d_ref[rows, :].reshape(SB // 8, 8, TILE) - dot[None])
+                probs.append(prob.reshape(SB, TILE).astype(BF16))
+                grads.append(grad.reshape(SB, TILE).astype(BF16))
             cs = slice(c * CHUNK, (c + 1) * CHUNK)
-            prob = e_ref[cs, :] * inv
-            grad = (prob * (dp_ref[cs, :] - dots)).astype(BF16)
+            prob, grad = jnp.concatenate(probs, axis=0), jnp.concatenate(grads, axis=0)
             ds[h, cs, ts] = grad
-            acc[cs, :] += jnp.dot(prob.astype(BF16), gzt, preferred_element_type=F32) + jnp.dot(grad, qzt, preferred_element_type=F32)
+            acc[cs, :] += jnp.dot(prob, gzt, preferred_element_type=F32) + jnp.dot(grad, qzt, preferred_element_type=F32)
+            yield
+
+    slot_a, slot_b = (e_a, d_a, m_a), (e_b, d_b, m_b)
+
+    def step(ahead, behind):
+        one = first_half(ahead[0], ahead[1], *ahead[2]) if ahead else None
+        two = second_half(behind[0], behind[1], *behind[2], dots[behind[3]]) if behind else None
+        for c in range(CHIPS):
+            if one:
+                next(one)
+            if two:
+                next(two)
+        if one:
+            dots[ahead[3]] = next(one)
+            next(one, None)
+
+    step((0, 0, slot_a, 0), None)
 
     def query_grad(h):
-        dqT[h] = jnp.dot(kT[h], ds[h], preferred_element_type=F32) * HD**-0.5
+        kT[...] = kv[h].reshape(SRC, 128).T[:HD]
+        dqT[h] = jnp.dot(kT[...], ds[h], preferred_element_type=F32) * HD**-0.5
 
     @pl.loop(0, HEADS)
     def _(h):
         acc[...] = jnp.zeros_like(acc)
 
-        @pl.loop(0, TGT // TILE)
-        def _(i):
-            @pl.when(i == 1)
+        @pl.loop(0, TILES // 2)
+        def _(u):
+            @pl.when(u == 1)
             def _():
                 @pl.when(h < HEADS - 1)
                 def _():
@@ -182,14 +229,19 @@
                 def _():
                     mid_step(h - 1)
 
-            tile(h, i)
-
-        part[h] = acc[...].astype(BF16).reshape(CHIPS, 2, SB, 128)
+            step((h, 2 * u + 1, slot_b, 1), (h, 2 * u, slot_a, 0))
+
+            @pl.when(jnp.logical_and(u == 1, h < HEADS - 1))
+            def _():
+                keys_ready(h + 1)
+
+            after = jnp.minimum(h * TILES + 2 * u + 2, HEADS * TILES - 1)
+            step((after // TILES, lax.rem(after, TILES), slot_a, 0), (h, 2 * u + 1, slot_b, 1))
+
+        both = acc[...].reshape(CHIPS, 2, SB, 128)
+        part[h] = both.astype(BF16)
+        own[...] = jnp.where(core == 0, both[:, 0], both[:, 1])
         to_sibling(h).start()
-
-        @pl.when(h < HEADS - 1)
-        def _():
-            keys_ready(h + 1)
 
     query_grad(0)
     mid_step(HEADS - 1)
@@ -222,16 +274,28 @@
         xs[r] = term((1 - xh) * NZ + z_at(r)).astype(BF16)
         across(r).start()
     for r in FAR_FIRST:
-        own = term(xh * NZ + z_at(r))
+        mine = term(xh * NZ + z_at(r))
         across(r).wait_recv()
-        own = own + xr[r].astype(F32)
+        mine = mine + xr[r].astype(F32)
+        if r in (3, 4, 5):
+            zs[r] = mine.astype(BF16)
+            relay(r).start()
+            continue
+        if r == 2:
+            relay(3).wait_recv()
+            relay(4).wait_recv()
+            far = zl[1].astype(F32)
+            mine = mine + zl[0].astype(F32) + jnp.where(core == 0, far, 0.0)
+        if r == 6:
+            relay(5).wait_recv()
+            mine = mine + zl[2].astype(F32) + jnp.where(core == 1, far, 0.0)
         if r:
-            zs[r] = own.astype(BF16)
+            zs[r] = mine.astype(BF16)
             along(r).start()
         else:
-            total = own
+            total = mine
     dq[...] = dqT[...].reshape(FEAT, TGT).T.astype(BF16)
-    for r in (1, 7, 2, 6, 3, 5, 4):
+    for r in NEAR:
         along(r).wait_recv()
         total = total + zr[r].astype(F32)
     mem[...] = total.astype(BF16)
@@ -244,8 +308,10 @@
         to_sibling(h).wait_send()
     for r in range(NZ):
         across(r).wait_send()
-        if r:
+        if r in NEAR:
             along(r).wait_send()
+        elif r:
+            relay(r).wait_send()
 
 
 def attention(lag, toff, soff, q, g, k, v, wk, wv):
@@ -263,11 +329,13 @@
             vmem((HEADS, TGT, 128), BF16),
             vmem((HEADS, TGT, 128), BF16),
             vmem((HEADS, CHIPS, 2, SB, 128), BF16),
-            vmem((HEADS, HD, SRC), BF16),
-            vmem((SRC, TILE), F32),
-            vmem((SRC, TILE), F32),
-            vmem((SRC, TILE), F32),
+            vmem((HD, SRC), BF16),
+        ]
+        + [vmem((SRC, TILE), F32), vmem((SRC, TILE), F32), vmem((2 * CHIPS, 8, TILE), F32)] * 2
+        + [
+            vmem((2, 8, TILE), F32),
             vmem((SRC, 128), F32),
+            vmem((CHIPS, SB, 128), F32),
             vmem((HEADS, SRC, TGT), BF16),
             vmem((HEADS, HD, TGT), F32),
             vmem((HEADS, CHIPS, 2, SB, 128), BF16),
@@ -278,18 +346,37 @@
             vmem((16 * COLS, FEAT), BF16),
         ]
         + [vmem((NZ, SB, COLS), BF16)] * 4
+        + [vmem((3, SB, COLS), BF16)]
         + [dma((HEADS, CHIPS))] * 2
         + [dma((HEADS,))] * 4
         + [dma((HEADS, CHIPS))] * 2
         + [dma((NZ,))] * 4
-        + [dma((2,))],
+        + [dma((3,)), dma((2,))],
         compiler_params=pltpu.CompilerParams(vmem_limit_bytes=58 * 2**20, collective_id=0, has_side_effects=True),
         name="wait_k_backward",
     )(lag, toff, soff, q, g, k, v, wk, wv)
 
 
+def hand_over_kernel(dq_in, mem_in, dq, mem):
+    dq[...] = dq_in[...]
+    mem[...] = mem_in[...]
+
+
+def hand_over(dq, mem):
+    vmem = pl.BlockSpec(memory_space=pltpu.VMEM)
+    return pl.pallas_call(
+        hand_over_kernel,
+        out_shape=(jax.ShapeDtypeStruct(dq.shape, dq.dtype), jax.ShapeDtypeStruct(mem.shape, mem.dtype)),
+        in_specs=[vmem, vmem],
+        out_specs=(vmem, vmem),
+        name="hand_over",
+    )(dq, mem)
+
+
 def body(queries, key_states, value_states, grad_out, key_weight, value_weight, wait_lag, target_offset, source_offset):
-    return attention(wait_lag, target_offset, source_offset, queries, grad_out, key_states, value_states, key_weight, value_weight)
+    return hand_over(
+        *attention(wait_lag, target_offset, source_offset, queries, grad_out, key_states, value_states, key_weight, value_weight)
+    )
 
 
 def solution(mesh):

time: 80.9 us -> 73.6 us (0.910)
  Pallas kernels: 75.4 us -> 70.9 us
  local copies, waits for them, and re-layouts: 3.34 us -> 0 us
    pallas_call x1, Pallas kernels: 75.4 us -> 69 us  [attention(): pl.pallas_call(kernel, out_shape=(jax.ShapeDtypeStruct((TGT, FEAT), BF16)...]
    unnamed x2 -> x0, local copies, waits for them, and re-layouts: 3.34 us -> none
    pallas_call x0 -> x1, Pallas kernels: none -> 1.88 us  [hand_over(): pl.pallas_call(hand_over_kernel, out_shape=(jax.ShapeDtypeStruct(dq.shape...]
where the time goes in v2:
time: 73.6 us; the launch traced here: 72.2 us
  Pallas kernels  70.9 us (96%)
  between operations  1.29 us (2%)
    pallas_call x1, Pallas kernels, attention(): pl.pallas_call(kernel, out_shape=(jax.ShapeDtypeStruct((TGT, FEAT), BF16)...  69 us
    pallas_call x1, Pallas kernels, hand_over(): pl.pallas_call(hand_over_kernel, out_shape=(jax.ShapeDtypeStruct(dq.shape...  1.88 us

profile of v2, /device:TPU:32, one launch (start us, length us, event | category | flops | bytes accessed | tf_op | source)
XLA Modules:
  0.0 72.2 jit_solution(17690748551680615723)
XLA Ops:
  1.3 69.0 %wait_k_backward.1 = (bf16[1024,256]{1,0:T(8,128)(2,1)}, bf16[128,256]{1,0:T(8,128)(2,1)}) custom-call(s32[1]{0:T(128)S(6)} %copy.11.lag, s32[16]{0:T(128)} %toff.1, s32[16]{0:T(128)} %soff.1, bf16[1024,256]{1,0:T(8,128)(2,1)} %q.1, bf16[1024,256]{1,0:T(8,128)(2,1)} %g.1, bf16[128,256]{1,0:T(8,128)(2,1)} %k.1, bf16[128,256]{1,0:T(8,128)(2,1)} %v.1, ...), custom_call_target="tpu_custom_call" | custom-call | tf_op jit(solution)/shard_map/wait_k_backward/pallas_call | solution.py:319
  70.3 1.9 %hand_over.1 = (bf16[1024,256]{1,0:T(8,128)(2,1)}, bf16[128,256]{1,0:T(8,128)(2,1)}) custom-call(bf16[1024,256]{1,0:T(8,128)(2,1)} %get-tuple-element.4.dq_in, bf16[128,256]{1,0:T(8,128)(2,1)} %get-tuple-element.5.mem_in), custom_call_target="tpu_custom_call" | custom-call | tf_op jit(solution)/shard_map/hand_over/pallas_call | solution.py:367

commit v3 on v2

--- a/solution.py
+++ b/solution.py
@@ -18,14 +18,15 @@
 CHIPS = SRC // CHUNK
 COLS = 256
 NZ = 8
-FAR_FIRST = (4, 3, 5, 2, 6, 1, 7, 0)
 NEAR = (1, 7, 2, 6)
+OWNERS = (5, 4, 3, 7, 2, 6, 1, 0)
+LAG = 5
 MESH = pl.DeviceIdType.MESH
 
 
-def kernel(lag, toff, soff, q, g, k, v, wk_hbm, wv_hbm, dq, mem,
-           qT, gT, qz, gz, kv, kT, e_a, d_a, m_a, e_b, d_b, m_b, dots, acc, own, ds, dqT, part, sib, mid, rs, wk, wv, xs, xr, zs, zr, zl,
-           ag_s, ag_r, fw_s, fw_r, sb_s, sb_r, rs_s, rs_r, x_s, x_r, z_s, z_r, l_r, w_sem):
+def kernel(lag, toff, soff, q_hbm, g_hbm, k_hbm, v_hbm, wk_hbm, wv_hbm, dq, mem,
+           q, g, k, v, qT, gT, qz, gz, kv, kT, e_a, d_a, m_a, e_b, d_b, m_b, dots, acc, own, ds, dqT, part, sib, mid, rs, wk, wv, xs, xr, zs, zr, zl, ys, yr,
+           ag_s, ag_r, fw_s, fw_r, sb_s, sb_r, rs_s, rs_r, x_s, x_r, z_s, z_r, l_r, w_sem, y_s, y_r, c_s, c_r):
     me, head = lax.axis_index("seq"), lax.axis_index("head")
     y, xl, core = me // 4, lax.rem(me // 2, 2), lax.rem(me, 2)
     chip = me // 2
@@ -45,9 +46,15 @@
     def z_peer(r):
         return (me, xh * NZ + z_at(r))
 
+    loads = [
+        pltpu.make_async_copy(src, dst, w_sem.at[n])
+        for n, (src, dst) in enumerate(((k_hbm, k), (v_hbm, v), (q_hbm, q), (g_hbm, g), (wk_hbm, wk), (wv_hbm, wv)))
+    ]
     barrier = pltpu.get_barrier_semaphore()
     for other in [sibling, partner] + [peer(r) for r in range(1, CHIPS)] + [z_peer(r) for r in NEAR]:
         pl.semaphore_signal(barrier, inc=1, device_id=other, device_id_type=MESH)
+    for load in loads:
+        load.start()
 
     def remote(src, dst, s_sem, r_sem, dev):
         return pltpu.make_async_remote_copy(src_ref=src, dst_ref=dst, send_sem=s_sem, recv_sem=r_sem, device_id=dev, device_id_type=MESH)
@@ -77,20 +84,20 @@
     def along(r):
         return remote(zs.at[r], zr.at[r], z_s.at[r], z_r.at[r], z_peer(r))
 
+    def along_too(r):
+        return remote(ys.at[r // 7], yr.at[r // 7], y_s.at[r // 7], y_r.at[r // 7], z_peer(r))
+
     def relay(r):
         step = 2 + 4 * core if r == 4 else 1 if r == 3 else 7
         return remote(zs.at[r], zl.at[r - 3], z_s.at[r], l_r.at[r - 3], z_peer(step))
 
-    load_k = pltpu.make_async_copy(wk_hbm, wk, w_sem.at[0])
-    load_v = pltpu.make_async_copy(wv_hbm, wv, w_sem.at[1])
-    load_k.start()
-    load_v.start()
-
     low = lax.broadcasted_iota(jnp.int32, (1, 128), 1) < HD
 
     def swapped(a):
         return jnp.concatenate([a[:, HD:], a[:, :HD]], axis=1)
 
+    loads[0].wait()
+    loads[1].wait()
     for p in range(HEADS // 2):
         kp, vp = k[:, p * 128 : (p + 1) * 128], v[:, p * 128 : (p + 1) * 128]
         kv[2 * p, chip, core] = jnp.where(low, kp, swapped(vp))
@@ -112,6 +119,8 @@
             gT[h, :HD, :] = zero
             gT[h, HD:, :] = gt[j * HD : (j + 1) * HD]
 
+    loads[2].wait()
+    loads[3].wait()
     prepare(0)
     pl.semaphore_wait(barrier, 13)
     for r in range(1, CHIPS):
@@ -193,6 +202,34 @@
             acc[cs, :] += jnp.dot(prob, gzt, preferred_element_type=F32) + jnp.dot(grad, qzt, preferred_element_type=F32)
             yield
 
+    def last_chunk(c, e_ref, d_ref, m_ref, dot):
+        ts = slice(TGT - TILE, TGT)
+        probs, grads = [], []
+        for b in range(2):
+            block = 2 * c + b
+            rows = pl.ds(pl.multiple_of(block * SB, SB), SB)
+            prob = e_ref[rows, :].reshape(SB // 8, 8, TILE) * m_ref[block][None]
+            grad = prob * (d_ref[rows, :].reshape(SB // 8, 8, TILE) - dot[None])
+            probs.append(prob.reshape(SB, TILE).astype(BF16))
+            grads.append(grad.reshape(SB, TILE).astype(BF16))
+        cs = pl.ds(pl.multiple_of(c * CHUNK, CHUNK), CHUNK)
+        prob, grad = jnp.concatenate(probs, axis=0), jnp.concatenate(grads, axis=0)
+        ds[HEADS - 1, cs, ts] = grad
+        value = jnp.dot(prob, gz[HEADS - 1, ts, :], preferred_element_type=F32)
+        value = value + jnp.dot(grad, qz[HEADS - 1, ts, :], preferred_element_type=F32)
+        return (acc[cs, :] + value).reshape(2, SB, 128)
+
+    def chunk_out(r):
+        c = chip_at(r, 1)
+        return remote(part.at[HEADS - 1, c, 1 - core], sib.at[HEADS - 1, c], c_s.at[r], c_r.at[r], sibling)
+
+    def pass_on(r):
+        c = chip_at(r, 1)
+        chunk_out(r).wait_recv()
+        mid[HEADS - 1, c] = (own[c] + sib[HEADS - 1, c].astype(F32)).astype(BF16)
+        if r:
+            scatter_out(HEADS - 1, r).start()
+
     slot_a, slot_b = (e_a, d_a, m_a), (e_b, d_b, m_b)
 
     def step(ahead, behind):
@@ -235,18 +272,32 @@
             def _():
                 keys_ready(h + 1)
 
-            after = jnp.minimum(h * TILES + 2 * u + 2, HEADS * TILES - 1)
-            step((after // TILES, lax.rem(after, TILES), slot_a, 0), (h, 2 * u + 1, slot_b, 1))
-
-        both = acc[...].reshape(CHIPS, 2, SB, 128)
-        part[h] = both.astype(BF16)
-        own[...] = jnp.where(core == 0, both[:, 0], both[:, 1])
-        to_sibling(h).start()
-
-    query_grad(0)
-    mid_step(HEADS - 1)
-
-    @pl.loop(1, HEADS)
+            after = h * TILES + 2 * u + 2
+
+            @pl.when(after < HEADS * TILES)
+            def _():
+                step((after // TILES, lax.rem(after, TILES), slot_a, 0), (h, 2 * u + 1, slot_b, 1))
+
+        @pl.when(h < HEADS - 1)
+        def _():
+            both = acc[...].reshape(CHIPS, 2, SB, 128)
+            part[h] = both.astype(BF16)
+            own[...] = jnp.where(core == 0, both[:, 0], both[:, 1])
+            to_sibling(h).start()
+
+    last = HEADS - 1
+    for n, r in enumerate(OWNERS):
+        c = chip_at(r, 1)
+        both = last_chunk(c, e_b, d_b, m_b, dots[1])
+        part[last, c] = both.astype(BF16)
+        own[c] = jnp.where(core == 0, both[0], both[1])
+        chunk_out(r).start()
+        if n >= LAG:
+            pass_on(OWNERS[n - LAG])
+    for r in OWNERS[CHIPS - LAG :]:
+        pass_on(r)
+
+    @pl.loop(0, HEADS)
     def _(h):
         query_grad(h)
 
@@ -260,8 +311,8 @@
 
     half_k = jnp.concatenate([jnp.where(low, half[2 * p], swapped(half[2 * p + 1])) for p in range(2)], axis=1).astype(BF16)
     half_v = jnp.concatenate([jnp.where(low, swapped(half[2 * p]), half[2 * p + 1]) for p in range(2)], axis=1).astype(BF16)
-    load_k.wait()
-    load_v.wait()
+    loads[4].wait()
+    loads[5].wait()
     contract = (((1,), (1,)), ((), ()))
 
     def term(index):
@@ -270,31 +321,48 @@
             half_v, wv[rows, :], contract, preferred_element_type=F32
         )
 
-    for r in FAR_FIRST:
+    def send_across(r):
         xs[r] = term((1 - xh) * NZ + z_at(r)).astype(BF16)
         across(r).start()
-    for r in FAR_FIRST:
+
+    for r in (4, 3, 5):
+        send_across(r)
+    for r in (1, 7):
+        zs[r] = term(xh * NZ + z_at(r)).astype(BF16)
+        along(r).start()
+        ys[r // 7] = term((1 - xh) * NZ + z_at(r)).astype(BF16)
+        along_too(r).start()
+    for r in (2, 6):
+        send_across(r)
+    for r in (4, 3, 5):
+        mine = term(xh * NZ + z_at(r))
+        across(r).wait_recv()
+        zs[r] = (mine + xr[r].astype(F32)).astype(BF16)
+        relay(r).start()
+    mine = term((1 - xh) * NZ + z)
+    for r in (1, 7):
+        along_too(r).wait_recv()
+        mine = mine + yr[r // 7].astype(F32)
+    xs[0] = mine.astype(BF16)
+    across(0).start()
+    for r in (2, 6):
         mine = term(xh * NZ + z_at(r))
         across(r).wait_recv()
         mine = mine + xr[r].astype(F32)
-        if r in (3, 4, 5):
-            zs[r] = mine.astype(BF16)
-            relay(r).start()
-            continue
         if r == 2:
             relay(3).wait_recv()
             relay(4).wait_recv()
             far = zl[1].astype(F32)
             mine = mine + zl[0].astype(F32) + jnp.where(core == 0, far, 0.0)
-        if r == 6:
+        else:
             relay(5).wait_recv()
             mine = mine + zl[2].astype(F32) + jnp.where(core == 1, far, 0.0)
-        if r:
-            zs[r] = mine.astype(BF16)
-            along(r).start()
-        else:
-            total = mine
+        zs[r] = mine.astype(BF16)
+        along(r).start()
+    total = term(xh * NZ + z)
     dq[...] = dqT[...].reshape(FEAT, TGT).T.astype(BF16)
+    across(0).wait_recv()
+    total = total + xr[0].astype(F32)
     for r in NEAR:
         along(r).wait_recv()
         total = total + zr[r].astype(F32)
@@ -305,13 +373,18 @@
             gather_out(h, r).wait_send()
             scatter_out(h, r).wait_send()
         forward(h).wait_send()
+    for h in range(HEADS - 1):
         to_sibling(h).wait_send()
-    for r in range(NZ):
+    for r in range(CHIPS):
+        chunk_out(r).wait_send()
+    for r in (0, 2, 3, 4, 5, 6):
         across(r).wait_send()
-        if r in NEAR:
-            along(r).wait_send()
-        elif r:
-            relay(r).wait_send()
+    for r in NEAR:
+        along(r).wait_send()
+    for r in (3, 4, 5):
+        relay(r).wait_send()
+    for r in (1, 7):
+        along_too(r).wait_send()
 
 
 def attention(lag, toff, soff, q, g, k, v, wk, wv):
@@ -320,10 +393,13 @@
         kernel,
         out_shape=(jax.ShapeDtypeStruct((TGT, FEAT), BF16), jax.ShapeDtypeStruct((SB, COLS), BF16)),
         in_specs=[pl.BlockSpec(memory_space=smem)] * 3
-        + [pl.BlockSpec(memory_space=vmem)] * 4
-        + [pl.BlockSpec(memory_space=pl.ANY)] * 2,
+        + [pl.BlockSpec(memory_space=pl.ANY)] * 6,
         out_specs=(pl.BlockSpec(memory_space=vmem),) * 2,
         scratch_shapes=[
+            vmem((TGT, FEAT), BF16),
+            vmem((TGT, FEAT), BF16),
+            vmem((SB, FEAT), BF16),
+            vmem((SB, FEAT), BF16),
             vmem((HEADS, 128, TGT), BF16),
             vmem((HEADS, 128, TGT), BF16),
             vmem((HEADS, TGT, 128), BF16),
@@ -347,11 +423,14 @@
         ]
         + [vmem((NZ, SB, COLS), BF16)] * 4
         + [vmem((3, SB, COLS), BF16)]
+        + [vmem((2, SB, COLS), BF16)] * 2
         + [dma((HEADS, CHIPS))] * 2
         + [dma((HEADS,))] * 4
         + [dma((HEADS, CHIPS))] * 2
         + [dma((NZ,))] * 4
-        + [dma((3,)), dma((2,))],
+        + [dma((3,)), dma((6,))]
+        + [dma((2,))] * 2
+        + [dma((CHIPS,))] * 2,
         compiler_params=pltpu.CompilerParams(vmem_limit_bytes=58 * 2**20, collective_id=0, has_side_effects=True),
         name="wait_k_backward",
     )(lag, toff, soff, q, g, k, v, wk, wv)

time: 73.6 us -> 69.8 us (0.948); the launches traced: 72.2 us -> 69.7 us
  Pallas kernels: 70.9 us -> 68.4 us
    pallas_call x1, Pallas kernels: 69 us -> 66.5 us  [attention(): pl.pallas_call(kernel, out_shape=(jax.ShapeDtypeStruct((TGT, FEAT), BF16)...]
where the time goes in v3:
time: 69.8 us; the launch traced here: 69.7 us
  Pallas kernels  68.4 us (98%)
  between operations  1.29 us (2%)
    pallas_call x1, Pallas kernels, attention(): pl.pallas_call(kernel, out_shape=(jax.ShapeDtypeStruct((TGT, FEAT), BF16)...  66.5 us
    pallas_call x1, Pallas kernels, hand_over(): pl.pallas_call(hand_over_kernel, out_shape=(jax.ShapeDtypeStruct(dq.shape...  1.88 us

profile of v3, /device:TPU:32, one launch (start us, length us, event | category | flops | bytes accessed | tf_op | source)
XLA Modules:
  0.0 69.7 jit_solution(5998020250430277598)
XLA Ops:
  1.3 66.5 %wait_k_backward.1 = (bf16[1024,256]{1,0:T(8,128)(2,1)}, bf16[128,256]{1,0:T(8,128)(2,1)}) custom-call(s32[1]{0:T(128)S(6)} %copy.11.lag, s32[16]{0:T(128)} %toff.1, s32[16]{0:T(128)} %soff.1, bf16[1024,256]{1,0:T(8,128)(2,1)} %q_hbm.1, bf16[1024,256]{1,0:T(8,128)(2,1)} %g_hbm.1, bf16[128,256]{1,0:T(8,128)(2,1)} %k_hbm.1, bf16[128,256]{1,0:T(8,128)(2,1)} %v_hbm.1, ...), custom_call_target="tpu_custom_call" | custom-call | tf_op jit(solution)/shard_map/wait_k_backward/pallas_call | solution.py:392
  67.8 1.9 %hand_over.1 = (bf16[1024,256]{1,0:T(8,128)(2,1)}, bf16[128,256]{1,0:T(8,128)(2,1)}) custom-call(bf16[1024,256]{1,0:T(8,128)(2,1)} %get-tuple-element.4.dq_in, bf16[128,256]{1,0:T(8,128)(2,1)} %get-tuple-element.5.mem_in), custom_call_target="tpu_custom_call" | custom-call | tf_op jit(solution)/shard_map/hand_over/pallas_call | solution.py:446

commit v4 on v3

--- a/solution.py
+++ b/solution.py
@@ -126,6 +126,8 @@
     for r in range(1, CHIPS):
         gather_out(0, r).start()
     prepare(1)
+    for r in range(1, CHIPS):
+        gather_out(1, r).start()
 
     def take_gathered(h):
         for r in range(1, CHIPS):
@@ -142,11 +144,6 @@
             scatter_out(h, r).start()
 
     take_gathered(0)
-
-    @pl.loop(1, HEADS)
-    def _(h):
-        for r in range(1, CHIPS):
-            gather_out(h, r).start()
 
     keys_ready(0)
 
@@ -252,6 +249,11 @@
 
     @pl.loop(0, HEADS)
     def _(h):
+        @pl.when(h < HEADS - 2)
+        def _():
+            for r in range(1, CHIPS):
+                gather_out(h + 2, r).start()
+
         acc[...] = jnp.zeros_like(acc)
 
         @pl.loop(0, TILES // 2)

time: 69.8 us -> 70.2 us (level)
  no operation moved by 1% of the time
where the time goes in v4:
time: 70.2 us; the launch traced here: 70.1 us
  Pallas kernels  68.8 us (98%)
  between operations  1.29 us (2%)
    pallas_call x1, Pallas kernels, attention(): pl.pallas_call(kernel, out_shape=(jax.ShapeDtypeStruct((TGT, FEAT), BF16)...  67 us
    pallas_call x1, Pallas kernels, hand_over(): pl.pallas_call(hand_over_kernel, out_shape=(jax.ShapeDtypeStruct(dq.shape...  1.88 us

profile of v4, /device:TPU:32, one launch (start us, length us, event | category | flops | bytes accessed | tf_op | source)
XLA Modules:
  0.0 70.1 jit_solution(17344227907234810395)
XLA Ops:
  1.3 67.0 %wait_k_backward.1 = (bf16[1024,256]{1,0:T(8,128)(2,1)}, bf16[128,256]{1,0:T(8,128)(2,1)}) custom-call(s32[1]{0:T(128)S(6)} %copy.11.lag, s32[16]{0:T(128)} %toff.1, s32[16]{0:T(128)} %soff.1, bf16[1024,256]{1,0:T(8,128)(2,1)} %q_hbm.1, bf16[1024,256]{1,0:T(8,128)(2,1)} %g_hbm.1, bf16[128,256]{1,0:T(8,128)(2,1)} %k_hbm.1, bf16[128,256]{1,0:T(8,128)(2,1)} %v_hbm.1, ...), custom_call_target="tpu_custom_call" | custom-call | tf_op jit(solution)/shard_map/wait_k_backward/pallas_call | solution.py:394
  68.2 1.9 %hand_over.1 = (bf16[1024,256]{1,0:T(8,128)(2,1)}, bf16[128,256]{1,0:T(8,128)(2,1)}) custom-call(bf16[1024,256]{1,0:T(8,128)(2,1)} %get-tuple-element.4.dq_in, bf16[128,256]{1,0:T(8,128)(2,1)} %get-tuple-element.5.mem_in), custom_call_target="tpu_custom_call" | custom-call | tf_op jit(solution)/shard_map/hand_over/pallas_call | solution.py:448

commit v5 on v4

--- a/solution.py
+++ b/solution.py
@@ -247,46 +247,44 @@
         kT[...] = kv[h].reshape(SRC, 128).T[:HD]
         dqT[h] = jnp.dot(kT[...], ds[h], preferred_element_type=F32) * HD**-0.5
 
-    @pl.loop(0, HEADS)
-    def _(h):
-        @pl.when(h < HEADS - 2)
+    @pl.loop(0, HEADS * TILES // 2 - 1)
+    def _(n):
+        h, u = n // 2, lax.rem(n, 2)
+
+        @pl.when(u == 0)
         def _():
-            for r in range(1, CHIPS):
-                gather_out(h + 2, r).start()
-
-        acc[...] = jnp.zeros_like(acc)
-
-        @pl.loop(0, TILES // 2)
-        def _(u):
-            @pl.when(u == 1)
+            @pl.when(h < HEADS - 2)
             def _():
-                @pl.when(h < HEADS - 1)
-                def _():
-                    take_gathered(h + 1)
-
-                @pl.when(h > 0)
-                def _():
-                    mid_step(h - 1)
-
-            step((h, 2 * u + 1, slot_b, 1), (h, 2 * u, slot_a, 0))
-
-            @pl.when(jnp.logical_and(u == 1, h < HEADS - 1))
+                for r in range(1, CHIPS):
+                    gather_out(h + 2, r).start()
+
+            @pl.when(h < HEADS - 1)
             def _():
-                keys_ready(h + 1)
-
-            after = h * TILES + 2 * u + 2
-
-            @pl.when(after < HEADS * TILES)
+                take_gathered(h + 1)
+
+            acc[...] = jnp.zeros_like(acc)
+
+        @pl.when(u == 1)
+        def _():
+            keys_ready(h + 1)
+
+            @pl.when(h > 0)
             def _():
-                step((after // TILES, lax.rem(after, TILES), slot_a, 0), (h, 2 * u + 1, slot_b, 1))
-
-        @pl.when(h < HEADS - 1)
+                mid_step(h - 1)
+
+        step((h, 2 * u + 1, slot_b, 1), (h, 2 * u, slot_a, 0))
+        after = 2 * n + 2
+        step((after // TILES, lax.rem(after, TILES), slot_a, 0), (h, 2 * u + 1, slot_b, 1))
+
+        @pl.when(u == 1)
         def _():
             both = acc[...].reshape(CHIPS, 2, SB, 128)
             part[h] = both.astype(BF16)
             own[...] = jnp.where(core == 0, both[:, 0], both[:, 1])
             to_sibling(h).start()
 
+    mid_step(HEADS - 2)
+    step((HEADS - 1, TILES - 1, slot_b, 1), (HEADS - 1, TILES - 2, slot_a, 0))
     last = HEADS - 1
     for n, r in enumerate(OWNERS):
         c = chip_at(r, 1)
@@ -309,19 +307,16 @@
         for r in range(1, CHIPS):
             scatter_out(h, r).wait_recv()
             total = total + rs[h, r].astype(F32)
-        half.append(total)
-
-    half_k = jnp.concatenate([jnp.where(low, half[2 * p], swapped(half[2 * p + 1])) for p in range(2)], axis=1).astype(BF16)
-    half_v = jnp.concatenate([jnp.where(low, swapped(half[2 * p]), half[2 * p + 1]) for p in range(2)], axis=1).astype(BF16)
+        half.append(total.T)
+
+    half_k = jnp.concatenate([t[:HD] for t in half], axis=0).astype(BF16)
+    half_v = jnp.concatenate([t[HD:] for t in half], axis=0).astype(BF16)
     loads[4].wait()
     loads[5].wait()
-    contract = (((1,), (1,)), ((), ()))
 
     def term(index):
         rows = pl.ds(pl.multiple_of(index * COLS, COLS), COLS)
-        return lax.dot_general(half_k, wk[rows, :], contract, preferred_element_type=F32) + lax.dot_general(
-            half_v, wv[rows, :], contract, preferred_element_type=F32
-        )
+        return jnp.dot(wk[rows, :], half_k, preferred_element_type=F32) + jnp.dot(wv[rows, :], half_v, preferred_element_type=F32)
 
     def send_across(r):
         xs[r] = term((1 - xh) * NZ + z_at(r)).astype(BF16)
@@ -368,7 +363,7 @@
     for r in NEAR:
         along(r).wait_recv()
         total = total + zr[r].astype(F32)
-    mem[...] = total.astype(BF16)
+    mem[...] = total.T.astype(BF16)
 
     for h in range(HEADS):
         for r in range(1, CHIPS):
@@ -423,9 +418,9 @@
             vmem((16 * COLS, FEAT), BF16),
             vmem((16 * COLS, FEAT), BF16),
         ]
-        + [vmem((NZ, SB, COLS), BF16)] * 4
-        + [vmem((3, SB, COLS), BF16)]
-        + [vmem((2, SB, COLS), BF16)] * 2
+        + [vmem((NZ, COLS, SB), BF16)] * 4
+        + [vmem((3, COLS, SB), BF16)]
+        + [vmem((2, COLS, SB), BF16)] * 2
         + [dma((HEADS, CHIPS))] * 2
         + [dma((HEADS,))] * 4
         + [dma((HEADS, CHIPS))] * 2

time: 70.2 us -> 68.8 us (0.980)
  Pallas kernels: 68.8 us -> 67.4 us
    pallas_call x1, Pallas kernels: 67 us -> 65.5 us  [attention(): pl.pallas_call(kernel, out_shape=(jax.ShapeDtypeStruct((TGT, FEAT), BF16)...]
where the time goes in v5:
time: 68.8 us; the launch traced here: 68.7 us
  Pallas kernels  67.4 us (98%)
  between operations  1.29 us (2%)
    pallas_call x1, Pallas kernels, attention(): pl.pallas_call(kernel, out_shape=(jax.ShapeDtypeStruct((TGT, FEAT), BF16)...  65.5 us
    pallas_call x1, Pallas kernels, hand_over(): pl.pallas_call(hand_over_kernel, out_shape=(jax.ShapeDtypeStruct(dq.shape...  1.88 us

profile of v5, /device:TPU:32, one launch (start us, length us, event | category | flops | bytes accessed | tf_op | source)
XLA Modules:
  0.0 68.7 jit_solution(3715178628937917611)
XLA Ops:
  1.3 65.5 %wait_k_backward.1 = (bf16[1024,256]{1,0:T(8,128)(2,1)}, bf16[128,256]{1,0:T(8,128)(2,1)}) custom-call(s32[1]{0:T(128)S(6)} %copy.11.lag, s32[16]{0:T(128)} %toff.1, s32[16]{0:T(128)} %soff.1, bf16[1024,256]{1,0:T(8,128)(2,1)} %q_hbm.1, bf16[1024,256]{1,0:T(8,128)(2,1)} %g_hbm.1, bf16[128,256]{1,0:T(8,128)(2,1)} %k_hbm.1, bf16[128,256]{1,0:T(8,128)(2,1)} %v_hbm.1, ...), custom_call_target="tpu_custom_call" | custom-call | tf_op jit(solution)/shard_map/wait_k_backward/pallas_call | solution.py:389
  66.8 1.9 %hand_over.1 = (bf16[1024,256]{1,0:T(8,128)(2,1)}, bf16[128,256]{1,0:T(8,128)(2,1)}) custom-call(bf16[1024,256]{1,0:T(8,128)(2,1)} %get-tuple-element.4.dq_in, bf16[128,256]{1,0:T(8,128)(2,1)} %get-tuple-element.5.mem_in), custom_call_target="tpu_custom_call" | custom-call | tf_op jit(solution)/shard_map/hand_over/pallas_call | solution.py:443

commit v6 on v5

--- a/solution.py
+++ b/solution.py
@@ -297,7 +297,7 @@
     for r in OWNERS[CHIPS - LAG :]:
         pass_on(r)
 
-    @pl.loop(0, HEADS)
+    @pl.loop(0, 2)
     def _(h):
         query_grad(h)
 
@@ -331,6 +331,7 @@
         along_too(r).start()
     for r in (2, 6):
         send_across(r)
+    query_grad(2)
     for r in (4, 3, 5):
         mine = term(xh * NZ + z_at(r))
         across(r).wait_recv()
@@ -342,6 +343,7 @@
         mine = mine + yr[r // 7].astype(F32)
     xs[0] = mine.astype(BF16)
     across(0).start()
+    query_grad(3)
     for r in (2, 6):
         mine = term(xh * NZ + z_at(r))
         across(r).wait_recv()

time: 68.8 us -> 68.9 us (level)
  no operation moved by 1% of the time
where the time goes in v6:
time: 68.9 us; the launch traced here: 68.7 us
  Pallas kernels  67.4 us (98%)
  between operations  1.29 us (2%)
    pallas_call x1, Pallas kernels, attention(): pl.pallas_call(kernel, out_shape=(jax.ShapeDtypeStruct((TGT, FEAT), BF16)...  65.5 us
    pallas_call x1, Pallas kernels, hand_over(): pl.pallas_call(hand_over_kernel, out_shape=(jax.ShapeDtypeStruct(dq.shape...  1.88 us

profile of v6, /device:TPU:32, one launch (start us, length us, event | category | flops | bytes accessed | tf_op | source)
XLA Modules:
  0.0 68.7 jit_solution(1022785562174924403)
XLA Ops:
  1.3 65.5 %wait_k_backward.1 = (bf16[1024,256]{1,0:T(8,128)(2,1)}, bf16[128,256]{1,0:T(8,128)(2,1)}) custom-call(s32[1]{0:T(128)S(6)} %copy.11.lag, s32[16]{0:T(128)} %toff.1, s32[16]{0:T(128)} %soff.1, bf16[1024,256]{1,0:T(8,128)(2,1)} %q_hbm.1, bf16[1024,256]{1,0:T(8,128)(2,1)} %g_hbm.1, bf16[128,256]{1,0:T(8,128)(2,1)} %k_hbm.1, bf16[128,256]{1,0:T(8,128)(2,1)} %v_hbm.1, ...), custom_call_target="tpu_custom_call" | custom-call | tf_op jit(solution)/shard_map/wait_k_backward/pallas_call | solution.py:391
  66.8 1.9 %hand_over.1 = (bf16[1024,256]{1,0:T(8,128)(2,1)}, bf16[128,256]{1,0:T(8,128)(2,1)}) custom-call(bf16[1024,256]{1,0:T(8,128)(2,1)} %get-tuple-element.4.dq_in, bf16[128,256]{1,0:T(8,128)(2,1)} %get-tuple-element.5.mem_in), custom_call_target="tpu_custom_call" | custom-call | tf_op jit(solution)/shard_map/hand_over/pallas_call | solution.py:445

commit v7 on v5

--- a/solution.py
+++ b/solution.py
@@ -119,12 +119,12 @@
             gT[h, :HD, :] = zero
             gT[h, HD:, :] = gt[j * HD : (j + 1) * HD]
 
+    pl.semaphore_wait(barrier, 13)
+    for r in range(1, CHIPS):
+        gather_out(0, r).start()
     loads[2].wait()
     loads[3].wait()
     prepare(0)
-    pl.semaphore_wait(barrier, 13)
-    for r in range(1, CHIPS):
-        gather_out(0, r).start()
     prepare(1)
     for r in range(1, CHIPS):
         gather_out(1, r).start()

time: 68.8 us -> 68.9 us (level)
  no operation moved by 1% of the time
where the time goes in v7:
time: 68.9 us; the launch traced here: 68.7 us
  Pallas kernels  67.4 us (98%)
  between operations  1.29 us (2%)
    pallas_call x1, Pallas kernels, attention(): pl.pallas_call(kernel, out_shape=(jax.ShapeDtypeStruct((TGT, FEAT), BF16)...  65.6 us
    pallas_call x1, Pallas kernels, hand_over(): pl.pallas_call(hand_over_kernel, out_shape=(jax.ShapeDtypeStruct(dq.shape...  1.88 us

profile of v7, /device:TPU:32, one launch (start us, length us, event | category | flops | bytes accessed | tf_op | source)
XLA Modules:
  0.0 68.7 jit_solution(478723502403411830)
XLA Ops:
  1.3 65.6 %wait_k_backward.1 = (bf16[1024,256]{1,0:T(8,128)(2,1)}, bf16[128,256]{1,0:T(8,128)(2,1)}) custom-call(s32[1]{0:T(128)S(6)} %copy.11.lag, s32[16]{0:T(128)} %toff.1, s32[16]{0:T(128)} %soff.1, bf16[1024,256]{1,0:T(8,128)(2,1)} %q_hbm.1, bf16[1024,256]{1,0:T(8,128)(2,1)} %g_hbm.1, bf16[128,256]{1,0:T(8,128)(2,1)} %k_hbm.1, bf16[128,256]{1,0:T(8,128)(2,1)} %v_hbm.1, ...), custom_call_target="tpu_custom_call" | custom-call | tf_op jit(solution)/shard_map/wait_k_backward/pallas_call | solution.py:389
  66.9 1.9 %hand_over.1 = (bf16[1024,256]{1,0:T(8,128)(2,1)}, bf16[128,256]{1,0:T(8,128)(2,1)}) custom-call(bf16[1024,256]{1,0:T(8,128)(2,1)} %get-tuple-element.4.dq_in, bf16[128,256]{1,0:T(8,128)(2,1)} %get-tuple-element.5.mem_in), custom_call_target="tpu_custom_call" | custom-call | tf_op jit(solution)/shard_map/hand_over/pallas_call | solution.py:443
